TPU v7x, 32 devices: a whole 2x2x4 slice. The times are simulated.
32 devices in a mesh: gx: 8 (over y, x, core), gy: 4 (over z).
Axes of the slice: x: 2, y: 2, z: 4, core: 2. Of those that a mesh axis runs over, the one named last changes fastest.
Arguments:
- node_latents: bfloat16 [8192, 128], P(('gx', 'gy')), may hold values from -6 to 6
- edge_latents: bfloat16 [8192, 64, 128], P(('gx', 'gy')), may hold values from -6 to 6
- node_cotangent: bfloat16 [8192, 128], P(('gx', 'gy')), may hold values from -6 to 6
- edge_cotangent: bfloat16 [8192, 64, 128], P(('gx', 'gy')), may hold values from -6 to 6
- neighbours: int32 [8192, 64], P(('gx', 'gy')), may hold values from 0 to 831, as said below
- edge_mask: int32 [8192, 64], P(('gx', 'gy')), may hold values from 0 to 1, as said below
- send_table: int32 [32, 64], P(('gx', 'gy')), may hold values from 0 to 255, as said below
- counts: int32 [32], P(('gx', 'gy')), may hold values from 85 to 256, as said below
- weights: float32 [9, 128, 128], replicated, may hold values from -0.375 to 0.375
- vectors: float32 [10, 128], replicated, may hold values from 0.1 to 1.9
- weights_m: float32 [9, 128, 128], replicated, may hold values from -0.010416667 to 0.010416667
- vectors_m: float32 [10, 128], replicated, may hold values from -0.041666668 to 0.041666668
- weights_v: float32 [9, 128, 128], replicated, may hold values from 6.781684e-06 to 2.7126736e-05
- vectors_v: float32 [10, 128], replicated, may hold values from 0.000108506945 to 0.00043402778
- weights_ema: float32 [9, 128, 128], replicated, may hold values from -0.375 to 0.375
- vectors_ema: float32 [10, 128], replicated, may hold values from 0.1 to 1.9
Outputs:
- nodes_out: bfloat16 [8192, 128], P(('gx', 'gy'))
- edges_out: bfloat16 [8192, 64, 128], P(('gx', 'gy'))
- nodes_grad: bfloat16 [8192, 128], P(('gx', 'gy'))
- edges_grad: bfloat16 [8192, 64, 128], P(('gx', 'gy'))
- grad_norm: float32 [], replicated
- weights_m_new: float32 [9, 128, 128], replicated
- vectors_m_new: float32 [10, 128], replicated
- weights_v_new: float32 [9, 128, 128], replicated
- vectors_v_new: float32 [10, 128], replicated
- weights_new: float32 [9, 128, 128], replicated
- vectors_new: float32 [10, 128], replicated
- weights_copy: bfloat16 [9, 128, 128], replicated
- vectors_copy: bfloat16 [10, 128], replicated
- weights_ema_new: float32 [9, 128, 128], replicated
- vectors_ema_new: float32 [10, 128], replicated
Inputs may be any that keep to these rules, and one draw needn't show every extreme that they name: `counts`: live particles of a device are its first rows; the last device is full. `edge_mask`: slot k of a particle is live when k is below its degree; each live particle has 1 to 60 live slots, dead particles none; some particle has 60. `neighbours`: a live slot names a live own row (0 to 255) or 256 + s * 64 + j, row j of halo slot s of a device inside the grid, never the centre slot s = 4; dead slots hold 0. `send_table`: distinct live rows of the device.
All inputs are finite; a program needn't handle non-finite values.
Results may differ from a plain program's by a relative error of at most 0.008.
Values may be sent and summed in bfloat16 or wider, within the bound.
No kernel may reach another device: no remote copies, remote signals or barrier semaphores. Data moves between devices by JAX's collectives and lax.ppermute only.
A program may use at most 128 MiB of HBM per device.

v0:
```python
import functools

import jax
import jax.numpy as jnp
from jax import lax
from jax.experimental import pallas as pl
from jax.experimental.pallas import tpu as pltpu
from jax.sharding import PartitionSpec as P

STEP = 10


first_decay = 0.5
second_decay = 0.5
adam_epsilon = 1e-08
weight_decay = 0.01
matrix_rate = 0.05
vector_rate = 0.2
average_decay = 0.9
clip_norm = 1.0
norm_epsilon = 1e-05


def neighbour_pairs(count):
    near = [(i, i ^ 1) for i in range(count) if (i ^ 1) < count]
    far = [(i, i + 1) for i in range(1, count - 1, 2)]
    return near, far + [(target, source) for source, target in far]


def stages(count):
    result, stride = [], 1
    while stride < count:
        factor = 2 if stride == 1 else min(4, count // stride)
        result.append((stride, factor))
        stride *= factor
    return result


def selector(indices, width, dtype):
    columns = lax.broadcasted_iota(jnp.int32, (indices.shape[0], width), 1)
    return (indices[:, None] == columns).astype(dtype)


def adamw(param, grad, moment, second, average, scale, rate):
    clipped = grad * scale
    moment_new = first_decay * moment + (1.0 - first_decay) * clipped
    second_new = second_decay * second + (1.0 - second_decay) * clipped * clipped
    corrected = moment_new / (1.0 - first_decay**STEP)
    denom = jnp.sqrt(second_new / (1.0 - second_decay**STEP)) + adam_epsilon
    param_new = param - rate * (corrected / denom + weight_decay * param)
    average_new = average_decay * average + (1.0 - average_decay) * param_new
    return (moment_new, second_new, param_new, average_new)


CHUNK = 16
GROUP = 32
UPDATE_ROWS = 32
TILE = CHUNK * GROUP
LANES = 128
PIECES = 8


def dot(left, right):
    return jnp.dot(left, right, preferred_element_type=jnp.float32)


def dot_nt(left, right):
    return lax.dot_general(
        left, right, (((1,), (1,)), ((), ())), preferred_element_type=jnp.float32
    )


def dot_tn(left, right):
    return lax.dot_general(
        left, right, (((0,), (0,)), ((), ())), preferred_element_type=jnp.float32
    )


def split_pair(values, axis=1):
    high = values.astype(jnp.bfloat16)
    low = (values - high.astype(jnp.float32)).astype(jnp.bfloat16)
    return jnp.concatenate([high, low], axis=axis)


def halves(pair):
    width = pair.shape[1] // 2
    return pair[:, :width] + pair[:, width:]


def silu_of_half(half):
    turn = jnp.tanh(half)
    lift = 1.0 + turn
    act = half * lift
    return act, lift + act * (1.0 - turn)


def row_sum(values):
    return jnp.sum(values, axis=-1, keepdims=True)


def scaled_unit(values, width):
    center = values - row_sum(values) * (1.0 / width)
    inverse = lax.rsqrt(row_sum(center * center) + width * norm_epsilon)
    return center * inverse, inverse


def scaled_unit_back(scaled, unit, inverse, width):
    shift = row_sum(scaled) * (1.0 / width)
    return inverse * (scaled - shift - unit * row_sum(scaled * unit))


def column_total(values):
    return jnp.sum(values, axis=0, keepdims=True)


def iota(shape, dim):
    return lax.broadcasted_iota(jnp.int32, shape, dim)


def slot_rows(quarter, halo):
    return (0, quarter, 2 * quarter + 3 * halo, 3 * quarter + 3 * halo)


def part_rows(relayed, side, slot, quarter):
    chip = lax.axis_index("gx") >> 1
    part = (chip + slot * (1 - 2 * side)) & 3 if relayed else slot
    return pl.ds(pl.multiple_of((side * 4 + part) * quarter, 16), quarter)


def plan_kernel(
    halo,
    count_ref,
    mask_hbm,
    neighbour_hbm,
    latents_hbm,
    vectors_hbm,
    upstream_hbm,
    weights_hbm,
    edges_hbm,
    latents_ref,
    vectors_ref,
    upstream_ref,
    edges_buf,
    list_rows,
    segment_ref,
    neighbour_rows,
    receiver_ref,
    low_ref,
    gather_ref,
    blocks_ref,
    mask_ref,
    neighbour_ref,
    weights_ref,
    sems,
):
    f32, bf16, i32 = jnp.float32, jnp.bfloat16, jnp.int32
    slots, particles = neighbour_ref.shape
    per = slots // CHUNK
    chunks = particles * per
    width = latents_ref.shape[1]
    rows = particles + 8 * halo
    fetches = [
        pltpu.make_async_copy(source, target, sems.at[order])
        for order, (source, target) in enumerate(
            (
                (mask_hbm, mask_ref),
                (neighbour_hbm, neighbour_ref),
                (latents_hbm, latents_ref),
                (vectors_hbm, vectors_ref),
                (weights_hbm, weights_ref),
                (upstream_hbm, upstream_ref),
            )
        )
    ]
    for copy in fetches:
        copy.start()
    piece = chunks // PIECES
    loads = [
        pltpu.make_async_copy(
            edges_hbm.at[pl.ds(p * piece, piece)],
            edges_buf.at[pl.ds(p * piece, piece)],
            sems.at[len(fetches) + p],
        )
        for p in range(PIECES)
    ]
    for copy in loads:
        copy.start()
    edges_buf[chunks] = jnp.zeros((CHUNK, width), bf16)
    fetches[0].wait()

    mask = mask_ref[...].astype(f32)
    degree = jnp.sum(mask, axis=0, keepdims=True)
    taken = ((degree.astype(i32) + (CHUNK - 1)) >> 4).astype(f32)
    earlier = iota((particles, particles), 0) < iota((particles, particles), 1)
    begin = dot(jnp.broadcast_to(taken, (16, particles)).astype(bf16), earlier.astype(bf16))
    degree_col = dot_tn(mask.astype(bf16), jnp.ones((slots, width), bf16))
    taken_col = ((degree_col.astype(i32) + (CHUNK - 1)) >> 4).astype(f32)
    later = iota((particles, particles), 1) < iota((particles, particles), 0)
    begin_col = dot(later.astype(bf16), taken_col.astype(bf16))
    end_col = begin_col + taken_col
    for block in range(chunks // width):
        lane = iota((particles, width), 1).astype(f32) + block * width
        segment_ref[:, block * width : (block + 1) * width] = (
            (lane >= begin_col) & (lane < end_col)
        ).astype(bf16)
    total = row_sum(taken)
    who = iota((16, particles), 1).astype(f32)
    offset = per * who - begin
    coarse = jnp.floor(offset * 0.125) * 8.0
    line = iota((16, particles), 0)
    facts = jnp.where(
        line == 0,
        who,
        jnp.where(line == 1, coarse, jnp.where(line == 2, offset - coarse, degree)),
    )
    listing = dot(facts.astype(bf16), segment_ref[...])
    place = iota((1, chunks), 1).astype(f32)
    particle = listing[0:1, :]
    chunk = listing[1:2, :] + listing[2:3, :] + place
    rest = listing[3:4, :] - CHUNK * (chunk - per * particle)
    used = place < total
    list_rows[...] = jnp.zeros(list_rows.shape, i32)
    list_rows[0:1, 0:chunks] = jnp.where(used, chunk, float(chunks)).astype(i32)
    list_rows[0:1, chunks:] = jnp.full((1, list_rows.shape[1] - chunks), chunks, i32)
    list_rows[1:2, 0:chunks] = jnp.where(used, particle, float(particles)).astype(i32)
    list_rows[1:2, chunks:] = jnp.full((1, list_rows.shape[1] - chunks), particles, i32)
    list_rows[2:3, 0:chunks] = jnp.where(used, rest, 0.0).astype(i32)
    list_rows[3:4, 0:particles] = jnp.broadcast_to(total, (1, particles)).astype(i32)
    list_rows[4:5, 0:particles] = (begin[0:1, :] + taken).astype(i32)
    list_rows[5:6, 0:particles] = jnp.full((1, particles), count_ref[0], i32)

    fetches[1].wait()
    neighbour = neighbour_ref[...]
    neighbour = jnp.where(neighbour >= particles + 5 * halo, neighbour - halo, neighbour)
    neighbour_rows[...] = jnp.zeros(neighbour_rows.shape, f32)
    neighbour_rows[0:particles, 0:slots] = neighbour.astype(f32).T

    block_of = iota((TILE, LANES), 0) >> 4
    for quarter in range(LANES // GROUP):
        blocks_ref[quarter] = (iota((TILE, LANES), 1) == block_of + quarter * GROUP).astype(bf16)

    for copy in fetches[2:]:
        copy.wait()
    for block in range(weights_ref.shape[0]):
        low_ref[block] = weights_ref[block].astype(bf16)
    for extra, block in ((9, 3), (10, 4)):
        low_ref[extra] = (0.5 * low_ref[block].astype(f32)).astype(bf16)
    latents = latents_ref[...]
    gather_ref[0:particles, :] = split_pair(0.5 * dot(latents, low_ref[2]))
    gather_ref[particles:rows, :] = jnp.zeros((rows - particles, 2 * width), bf16)
    gather_ref[rows : rows + width, :] = jnp.concatenate(
        [(0.5 * low_ref[0].astype(f32)).astype(bf16), jnp.zeros((width, width), bf16)], axis=1
    )
    gather_ref[rows + width :, :] = jnp.zeros((LANES, 2 * width), bf16)
    receiver_ref[0:particles, :] = 0.5 * (dot(latents, low_ref[1]) + vectors_ref[0:1, :])
    receiver_ref[particles:, :] = jnp.zeros((receiver_ref.shape[0] - particles, width), f32)
    for copy in loads:
        copy.wait()


def layer_kernel(
    halo,
    relayed,
    latents_ref,
    ring_ref,
    ring_far_ref,
    ring_near_ref,
    upstream_ref,
    vectors_ref,
    list_rows,
    segment_ref,
    neighbour_rows,
    receiver_ref,
    low_ref,
    blocks_ref,
    edges_in,
    gather_in,
    cotangent_hbm,
    nodes_out_hbm,
    edges_out_hbm,
    edges_grad_hbm,
    node_part_ref,
    halo_own_ref,
    send_ref,
    keep_ref,
    edges_buf,
    gather_ref,
    nodes_out_ref,
    cotangent_buf,
    kept_edges,
    kept_index,
    kept_act1,
    kept_act2,
    kept_slope1,
    kept_slope2,
    kept_unit,
    kept_inverse,
    table_ref,
    descent_ref,
    receiver_tile,
    chunk_sums,
    chunk_grads,
    index_acc,
    mat_acc,
    vec_acc,
    first_tile,
    last_tile,
    third_tile,
    first_back,
    second_back,
    passed_tile,
    halo_grad,
    grads,
    listed,
    in_sems,
    out_sems,
    list_sem,
    nodes_sem,
):
    f32, bf16, i32 = jnp.float32, jnp.bfloat16, jnp.int32
    fetch_list = pltpu.make_async_copy(list_rows, listed, list_sem)
    fetch_list.start()
    particles, chunks = segment_ref.shape
    per = chunks // particles
    width = latents_ref.shape[1]
    rows = table_ref.shape[0]
    piece = chunks // PIECES
    root = float(width) ** 0.5
    odd_x = lax.axis_index("gx") & 1
    odd_y = lax.axis_index("gy") & 1
    loads = [
        pltpu.make_async_copy(
            cotangent_hbm.at[pl.ds(p * piece, piece)],
            cotangent_buf.at[pl.ds(p * piece, piece)],
            in_sems.at[p],
        )
        for p in range(PIECES)
    ]
    for copy in loads:
        copy.start()
    cotangent_buf[chunks] = jnp.zeros((CHUNK, width), bf16)

    table_ref[0:particles, :] = latents_ref[...]
    far, near, own = ring_far_ref[...], ring_near_ref[...], ring_ref[...]
    low_y = jnp.where(odd_y == 0, far, near)
    high_y = jnp.where(odd_y == 0, near, far)
    spot = particles
    for a in range(3):
        for b, strip in enumerate((low_y, own, high_y)):
            if a == 1 and b == 1:
                continue
            if a == 1:
                part = strip[2 * halo :]
            elif a == 0:
                part = jnp.where(odd_x == 0, strip[0:halo], strip[halo : 2 * halo])
            else:
                part = jnp.where(odd_x == 0, strip[halo : 2 * halo], strip[0:halo])
            table_ref[spot : spot + halo, :] = part
            spot += halo

    vectors = vectors_ref[...]

    def vector(row):
        return vectors[row : row + 1, :]

    latents = latents_ref[...]
    half3, half4 = low_ref[9], low_ref[10]
    gather_ref[particles:rows, :] = split_pair(0.5 * dot(table_ref[particles:, :], low_ref[2]))
    chunk_sums[...] = jnp.zeros(chunk_sums.shape, f32)
    chunk_grads[...] = jnp.zeros(chunk_grads.shape, f32)
    index_acc[...] = jnp.zeros(index_acc.shape, f32)
    mat_acc[...] = jnp.zeros(mat_acc.shape, f32)
    vec_acc[...] = jnp.zeros(vec_acc.shape, f32)
    tail = 9 * width
    grads[tail:, :] = jnp.zeros((grads.shape[0] - tail, width), f32)
    descent_ref[particles:, :] = jnp.zeros((descent_ref.shape[0] - particles, width), f32)

    fetch_list.wait()
    tiles = (listed[3, 0] + (GROUP - 1)) >> 5

    sublane = iota((CHUNK, width), 0)
    diagonal = iota((CHUNK, width), 1) - sublane
    lane16 = iota((TILE, width), 1).astype(jnp.int16)

    def flat(ref, t):
        return ref[pl.ds(t * GROUP, GROUP)].reshape(TILE, width)

    def keep(ref, t, values):
        ref[pl.ds(t * GROUP, GROUP)] = values.astype(ref.dtype).reshape(GROUP, CHUNK, width)

    def span(j):
        return slice(j * CHUNK, (j + 1) * CHUNK)

    def one_hot(t):
        index = flat(kept_index, t)
        return [
            jnp.where(index == lane16 + jnp.int16(b * width), bf16(1), bf16(0))
            for b in range(rows // width)
        ]

    def gather(t):
        base = t * GROUP
        for j in range(GROUP):
            chunk, particle = listed[0, base + j], listed[1, base + j]
            kept_edges[base + j] = edges_buf[chunk]
            row = jnp.broadcast_to(neighbour_rows[pl.ds(particle, 1), :], (CHUNK, width))
            start = (chunk & (per - 1)) * CHUNK
            index = row_sum(jnp.where(diagonal == start, row, 0.0))
            kept_index[base + j] = (
                jnp.broadcast_to(index, (CHUNK, width)).astype(i32).astype(jnp.int16)
            )
            receiver_tile[j : j + 1, :] = receiver_ref[pl.ds(particle, 1), :]
        gather_ref[rows + width : rows + width + GROUP, :] = split_pair(receiver_tile[...])

    def project(t):
        picks = jnp.concatenate(one_hot(t) + [flat(kept_edges, t), blocks_ref[0]], axis=1)
        first_tile[...] = halves(dot(picks, gather_ref[...]))

    gain_root = vector(3) * root

    def finish(t):
        base = t * GROUP
        unit, inverse = scaled_unit(last_tile[...], width)
        keep(kept_unit, t, unit)
        keep(kept_inverse, t, jnp.broadcast_to(inverse, (TILE, width)))
        change = unit * gain_root + vector(4)
        for j in range(GROUP):
            chunk = listed[0, base + j]
            alive = sublane < listed[2, base + j]
            fresh = kept_edges[base + j].astype(f32) + jnp.where(alive, change[span(j)], 0.0)
            edges_buf[chunk] = fresh.astype(bf16)
            chunk_sums[pl.ds(base + j, 1), :] = column_total(jnp.where(alive, fresh, 0.0))

    def forward(t, carry):
        gather(t + 1)
        act, slope = silu_of_half(first_tile[...])
        act = act.astype(bf16)
        keep(kept_act1, t, act)
        keep(kept_slope1, t, slope)
        finish(jnp.where(t == 0, tiles, t - 1))
        act, slope = silu_of_half(dot(act, half3) + 0.5 * vector(1))
        act = act.astype(bf16)
        keep(kept_act2, t, act)
        keep(kept_slope2, t, slope)
        project(t + 1)
        last_tile[...] = dot(act, low_ref[4]) + vector(2)
        return carry

    for ref in (kept_act1, kept_edges):
        keep(ref, tiles, jnp.zeros((TILE, width), f32))
    last_tile[...] = jnp.zeros(last_tile.shape, f32)
    gather(0)
    project(0)
    lax.fori_loop(0, tiles, forward, 0)
    finish(jnp.where(tiles == 0, tiles, tiles - 1))

    stores = [
        pltpu.make_async_copy(
            edges_buf.at[pl.ds(p * piece, piece)],
            edges_out_hbm.at[pl.ds(p * piece, piece)],
            out_sems.at[p],
        )
        for p in range(PIECES)
    ]
    for copy in stores:
        copy.start()

    aggregate = halves(dot(segment_ref[...], split_pair(chunk_sums[0:chunks, :]))).astype(bf16)
    half1 = 0.5 * (dot(latents, low_ref[5]) + dot(aggregate, low_ref[6]) + vector(5))
    act1, slope1 = silu_of_half(half1)
    act1 = act1.astype(bf16)
    act2, slope2 = silu_of_half(0.5 * (dot(act1, low_ref[7]) + vector(6)))
    act2 = act2.astype(bf16)
    unit, inverse = scaled_unit(dot(act2, low_ref[8]) + vector(7), width)
    alive = (iota((particles, width), 0) < listed[5, 0]).astype(f32)
    upstream = upstream_ref[...].astype(f32)
    nodes_out_ref[...] = (
        latents.astype(f32) + alive * (unit * (vector(8) * root) + vector(9))
    ).astype(bf16)
    send_nodes = pltpu.make_async_copy(nodes_out_ref, nodes_out_hbm, nodes_sem)
    send_nodes.start()
    held = alive * upstream
    third = scaled_unit_back(held * (vector(8) * root), unit, inverse, width).astype(bf16)
    second = (0.5 * slope2 * dot_nt(third, low_ref[8])).astype(bf16)
    first = (0.5 * slope1 * dot_nt(second, low_ref[7])).astype(bf16)
    descent_ref[0:particles, :] = dot_nt(first, low_ref[6])
    node_part_ref[...] = upstream + dot_nt(first, low_ref[5])

    def put_block(block, values):
        grads[block * width : (block + 1) * width, :] = values

    put_block(5, dot_tn(latents, first))
    put_block(6, dot_tn(aggregate, first))
    put_block(7, dot_tn(act1, second))
    put_block(8, dot_tn(act2, third))
    for row, values in enumerate(
        (first.astype(f32), second.astype(f32), third.astype(f32), held * unit * root, held)
    ):
        grads[tail + 5 + row : tail + 6 + row, :] = column_total(values)

    for copy in loads:
        copy.wait()

    def add_columns(row, values):
        vec_acc[8 * row : 8 * row + 8, :] += jnp.sum(values.reshape(TILE // 8, 8, width), axis=0)

    def accept(t):
        base = t * GROUP
        parts = []
        for j in range(GROUP):
            chunk, particle = listed[0, base + j], listed[1, base + j]
            alive = sublane < listed[2, base + j]
            passed = cotangent_buf[chunk].astype(f32) + jnp.where(
                alive, descent_ref[pl.ds(particle, 1), :], 0.0
            )
            passed_tile[t & 3, span(j), :] = passed
            parts.append(jnp.where(alive, passed, 0.0))
        return jnp.concatenate(parts, axis=0)

    def descend(t, held):
        unit = flat(kept_unit, t).astype(f32)
        third = scaled_unit_back(held * gain_root, unit, flat(kept_inverse, t), width)
        third_tile[...] = third.astype(bf16)
        add_columns(2, third)
        add_columns(3, held * unit)
        add_columns(4, held)

    def settle(t, slot):
        base = t * GROUP
        first = first_back[...]
        result = passed_tile[slot] + dot_nt(first, low_ref[0])
        for j in range(GROUP):
            cotangent_buf[listed[0, base + j]] = result[span(j)].astype(bf16)
        picks = jnp.concatenate(one_hot(t) + [flat(kept_edges, t), blocks_ref[t & 3]], axis=1)
        index_acc[...] += dot_tn(first, picks[:, 0 : rows + width])
        chunk_grads[t >> 2] += dot_tn(first, picks[:, rows + width :])
        mat_acc[0] += dot_tn(flat(kept_act1, t), second_back[...])

    def backward(t, carry):
        third = third_tile[...]
        second = dot_nt(third, half4)
        held = accept(t + 1)
        settle(jnp.where(t == 0, tiles, t - 1), (t + 3) & 3)
        second = flat(kept_slope2, t).astype(f32) * second
        add_columns(1, second)
        second = second.astype(bf16)
        descend(t + 1, held)
        first = flat(kept_slope1, t).astype(f32) * dot_nt(second, half3)
        mat_acc[1] += dot_tn(flat(kept_act2, t), third)
        first_back[...] = first.astype(bf16)
        second_back[...] = second
        return carry

    first_back[...] = jnp.zeros(first_back.shape, bf16)
    second_back[...] = jnp.zeros(second_back.shape, bf16)
    passed_tile[3] = jnp.zeros((TILE, width), f32)
    descend(0, accept(0))
    def send_piece(p):
        pltpu.make_async_copy(
            cotangent_buf.at[pl.ds(p * piece, piece)],
            edges_grad_hbm.at[pl.ds(p * piece, piece)],
            out_sems.at[PIECES + p],
        ).start()

    def last_tile(p):
        return (listed[4, (p + 1) * (piece // per) - 1] + (GROUP - 1)) >> 5

    def backward_piece(p, t):
        upto = last_tile(p) + 1
        stop = jnp.minimum(upto, tiles)
        lax.fori_loop(t, stop, backward, 0)

        @pl.when(upto <= tiles)
        def _():
            send_piece(p)

        return jnp.maximum(t, stop)

    lax.fori_loop(0, PIECES, backward_piece, jnp.int32(0))
    settle(jnp.where(tiles == 0, tiles, tiles - 1), (tiles + 3) & 3)

    @pl.loop(0, PIECES)
    def _(p):
        @pl.when(last_tile(p) + 1 > tiles)
        def _():
            send_piece(p)

    stacked = split_pair(
        jnp.concatenate([chunk_grads[g] for g in range(chunks // LANES)], axis=1), axis=0
    )
    receiver_grad = halves(dot_nt(segment_ref[...], stacked)).astype(bf16)
    grads[tail : tail + 1, :] = halves(dot_nt(jnp.ones((8, chunks), bf16), stacked))[0:1, :]
    for row in range(1, 5):
        values = column_total(vec_acc[8 * row : 8 * row + 8, :])
        grads[tail + row : tail + row + 1, :] = values * root if row == 3 else values
    sent = index_acc[:, 0:rows].astype(bf16)
    put_block(0, index_acc[:, rows:].T)
    put_block(1, dot_tn(latents, receiver_grad))
    put_block(2, dot(sent, table_ref[...]).T)
    put_block(3, mat_acc[0])
    put_block(4, mat_acc[1])
    table_grad = lax.dot_general(
        sent, low_ref[2], (((0,), (1,)), ((), ())), preferred_element_type=f32
    )
    node_part_ref[...] += dot_nt(receiver_grad, low_ref[1]) + table_grad[0:particles, :]
    halo_grad[...] = table_grad[particles:, :].astype(bf16)
    low_x = halo_grad[0 : 3 * halo, :]
    high_x = halo_grad[5 * halo : 8 * halo, :]
    halo_own_ref[0:halo, :] = halo_grad[3 * halo : 4 * halo, :]
    halo_own_ref[halo : 2 * halo, :] = jnp.zeros((halo, width), bf16)
    halo_own_ref[2 * halo :, :] = halo_grad[4 * halo : 5 * halo, :]
    quarter = grads.shape[0] // 8
    relay = 2 * quarter
    send_ref[relay : relay + 3 * halo, :] = jnp.where(odd_x == 0, low_x, high_x)
    send_ref[4 * quarter + 3 * halo :, :] = jnp.where(odd_x == 0, high_x, low_x)
    keep_ref[relay : relay + 3 * halo, :] = jnp.zeros((3 * halo, width), f32)
    for slot, spot in enumerate(slot_rows(quarter, halo)):
        kept_rows = part_rows(relayed, odd_x, slot, quarter)
        sent_rows = part_rows(relayed, 1 - odd_x, slot, quarter)
        keep_ref[spot : spot + quarter, :] = grads[kept_rows, :]
        send_ref[spot : spot + quarter, :] = grads[sent_rows, :].astype(bf16)

    for copy in stores + [send_nodes]:
        copy.wait()
    for p in range(PIECES):
        pltpu.make_async_copy(
            cotangent_buf.at[pl.ds(p * piece, piece)],
            edges_grad_hbm.at[pl.ds(p * piece, piece)],
            out_sems.at[PIECES + p],
        ).wait()


def pinned(values):
    return pltpu.with_memory_space_constraint(values, pltpu.VMEM)


def outer(values):
    return pltpu.with_memory_space_constraint(values, pltpu.HBM)


def plan_call(halo, counts, neighbours, edge_mask, latents, vectors, upstream, weights, edges):
    f32, bf16, i32 = jnp.float32, jnp.bfloat16, jnp.int32
    particles, slots = neighbours.shape
    width = latents.shape[1]
    chunks = particles * slots // CHUNK
    whole = pl.BlockSpec(memory_space=pltpu.VMEM)
    outside = pl.BlockSpec(memory_space=pl.ANY)
    return pl.pallas_call(
        functools.partial(plan_kernel, halo),
        out_shape=(
            pltpu.VMEM(latents.shape, bf16),
            pltpu.VMEM(vectors.shape, f32),
            pltpu.VMEM(upstream.shape, bf16),
            pltpu.VMEM((chunks + 1, CHUNK, width), bf16),
            pltpu.VMEM((8, chunks + LANES), i32),
            pltpu.VMEM((particles, chunks), bf16),
            pltpu.VMEM((particles + 8, width), f32),
            pltpu.VMEM((particles + 8, width), f32),
            pltpu.VMEM((weights.shape[0] + 2, width, width), bf16),
            pltpu.VMEM((particles + 8 * halo + width + LANES, 2 * width), bf16),
            pltpu.VMEM((LANES // GROUP, TILE, LANES), bf16),
        ),
        in_specs=[pl.BlockSpec(memory_space=pltpu.SMEM)] + [outside] * 7,
        out_specs=(whole,) * 11,
        scratch_shapes=[
            pltpu.VMEM((slots, particles), i32),
            pltpu.VMEM((slots, particles), i32),
            pltpu.VMEM(weights.shape, f32),
            pltpu.SemaphoreType.DMA((6 + PIECES,)),
        ],
        compiler_params=pltpu.CompilerParams(vmem_limit_bytes=16 * 1024 * 1024),
        cost_estimate=pl.CostEstimate(
            flops=10**9, bytes_accessed=12 * 10**6, transcendentals=0
        ),
        name="plan",
    )(
        counts,
        outer(edge_mask.T),
        outer(neighbours.T),
        outer(latents),
        outer(vectors),
        outer(upstream),
        outer(weights),
        outer(edges),
    )


def layer_call(halo, relayed, grad_rows, ring, ring_far, ring_near, cotangents, plan):
    f32, bf16, i32 = jnp.float32, jnp.bfloat16, jnp.int32
    latents, vectors, upstream, edges, listing, segment, *more, gather, blocks = plan
    neighbour_rows, receiver, low = more
    particles, chunks = segment.shape
    width = latents.shape[1]
    rows = particles + 8 * halo
    whole = pl.BlockSpec(memory_space=pltpu.VMEM)
    outside = pl.BlockSpec(memory_space=pl.ANY)
    edge_shape = (chunks, CHUNK, width)
    kept_shape = (chunks + GROUP, CHUNK, width)
    kept = pltpu.VMEM(kept_shape, bf16)
    half = grad_rows // 2
    return pl.pallas_call(
        functools.partial(layer_kernel, halo, relayed),
        out_shape=(
            jax.ShapeDtypeStruct((particles, width), bf16),
            jax.ShapeDtypeStruct(edge_shape, bf16),
            jax.ShapeDtypeStruct(edge_shape, bf16),
            pltpu.VMEM((particles, width), f32),
            pltpu.VMEM((3 * halo, width), bf16),
            pltpu.VMEM((half + 6 * halo, width), bf16),
            pltpu.VMEM((half + 3 * halo, width), f32),
            pltpu.VMEM(edges.shape, bf16),
            pltpu.VMEM(gather.shape, bf16),
        ),
        in_specs=[whole] * 14 + [outside],
        out_specs=(outside,) * 3 + (whole,) * 6,
        input_output_aliases={12: 7, 13: 8},
        scratch_shapes=[
            pltpu.VMEM((particles, width), bf16),
            pltpu.VMEM(edges.shape, bf16),
            kept,
            pltpu.VMEM(kept_shape, jnp.int16),
            kept,
            kept,
            kept,
            kept,
            kept,
            pltpu.VMEM(kept_shape, f32),
            pltpu.VMEM((rows, width), bf16),
            pltpu.VMEM((particles + 8, width), f32),
            pltpu.VMEM((GROUP, width), f32),
            pltpu.VMEM((chunks + GROUP, width), f32),
            pltpu.VMEM((chunks // LANES + 1, width, LANES), f32),
            pltpu.VMEM((width, rows + width), f32),
            pltpu.VMEM((2, width, width), f32),
            pltpu.VMEM((40, width), f32),
            pltpu.VMEM((TILE, width), f32),
            pltpu.VMEM((TILE, width), f32),
            pltpu.VMEM((TILE, width), bf16),
            pltpu.VMEM((TILE, width), bf16),
            pltpu.VMEM((TILE, width), bf16),
            pltpu.VMEM((4, TILE, width), f32),
            pltpu.VMEM((8 * halo, width), bf16),
            pltpu.VMEM((grad_rows, width), f32),
            pltpu.SMEM((8, chunks + LANES), i32),
            pltpu.SemaphoreType.DMA((PIECES,)),
            pltpu.SemaphoreType.DMA((2 * PIECES,)),
            pltpu.SemaphoreType.DMA,
            pltpu.SemaphoreType.DMA,
        ],
        compiler_params=pltpu.CompilerParams(vmem_limit_bytes=52 * 1024 * 1024),
        name="edge_layer",
    )(
        pinned(latents),
        pinned(ring),
        pinned(ring_far),
        pinned(ring_near),
        pinned(upstream),
        pinned(vectors),
        pinned(listing),
        pinned(segment),
        pinned(neighbour_rows),
        pinned(receiver),
        pinned(low),
        pinned(blocks),
        pinned(edges),
        pinned(gather),
        outer(cotangents),
    )[:7]


def update_kernel(
    relayed,
    mine_ref,
    other_ref,
    weights_ref,
    vectors_ref,
    weights_m_ref,
    vectors_m_ref,
    weights_v_ref,
    vectors_v_ref,
    weights_ema_ref,
    vectors_ema_ref,
    norm_ref,
    weights_m_out,
    vectors_m_out,
    weights_v_out,
    vectors_v_out,
    weights_out,
    vectors_out,
    weights_copy_out,
    vectors_copy_out,
    weights_ema_out,
    vectors_ema_out,
    grads,
):
    f32 = jnp.float32
    odd = lax.axis_index("gx") & 1
    half_rows, width = mine_ref.shape
    quarter = half_rows // 4
    squares = jnp.zeros((8, width), f32)
    for side, part_ref in ((odd, mine_ref), (1 - odd, other_ref)):
        for slot in range(4):
            values = part_ref[slot * quarter : (slot + 1) * quarter, :].astype(f32)
            grads[part_rows(relayed, side, slot, quarter), :] = values
            squares = squares + jnp.sum((values * values).reshape(quarter // 8, 8, width), axis=0)
    norm = jnp.sqrt(jnp.sum(jnp.sum(squares, axis=1, keepdims=True), axis=0, keepdims=True))
    norm_ref[...] = norm
    scale = clip_norm / jnp.maximum(norm, clip_norm)
    for block in range(weights_ref.shape[0]):
        for row in range(0, width, UPDATE_ROWS):
            part = slice(row, row + UPDATE_ROWS)
            moment, second, param, average = adamw(
                weights_ref[block, part, :],
                grads[block * width + row : block * width + row + UPDATE_ROWS, :],
                weights_m_ref[block, part, :],
                weights_v_ref[block, part, :],
                weights_ema_ref[block, part, :],
                scale,
                matrix_rate,
            )
            weights_m_out[block, part, :] = moment
            weights_v_out[block, part, :] = second
            weights_out[block, part, :] = param
            weights_copy_out[block, part, :] = param.astype(jnp.bfloat16)
            weights_ema_out[block, part, :] = average
    tail = weights_ref.shape[0] * width
    moment, second, param, average = adamw(
        vectors_ref[...],
        grads[tail : tail + vectors_ref.shape[0], :],
        vectors_m_ref[...],
        vectors_v_ref[...],
        vectors_ema_ref[...],
        scale,
        vector_rate,
    )
    vectors_m_out[...] = moment
    vectors_v_out[...] = second
    vectors_out[...] = param
    vectors_copy_out[...] = param.astype(jnp.bfloat16)
    vectors_ema_out[...] = average


def update_call(relayed, mine, other, weights, vectors, weights_m, vectors_m, weights_v, vectors_v,
                weights_ema, vectors_ema):
    f32, bf16 = jnp.float32, jnp.bfloat16
    mat, vec = weights.shape, vectors.shape
    kinds = (
        ((1, 1), f32), (mat, f32), (vec, f32), (mat, f32), (vec, f32), (mat, f32), (vec, f32),
        (mat, bf16), (vec, bf16), (mat, f32), (vec, f32),
    )
    whole = pl.BlockSpec(memory_space=pltpu.VMEM)
    return pl.pallas_call(
        functools.partial(update_kernel, relayed),
        out_shape=tuple(jax.ShapeDtypeStruct(*kind) for kind in kinds),
        in_specs=[whole] * 10,
        out_specs=(whole,) * 11,
        scratch_shapes=[pltpu.VMEM((2 * mine.shape[0], mine.shape[1]), f32)],
        compiler_params=pltpu.CompilerParams(vmem_limit_bytes=24 * 1024 * 1024),
        name="update",
    )(mine, other, weights, vectors, weights_m, vectors_m, weights_v, vectors_v, weights_ema,
      vectors_ema)


def pair_exchange(to_far, to_near, axis):
    near, far = neighbour_pairs(lax.axis_size(axis))
    return lax.ppermute(to_far, axis, far), lax.ppermute(to_near, axis, near)


def partners(axis, stride, mask):
    return [(i, i ^ (mask * stride)) for i in range(lax.axis_size(axis))]


def even_pick(axis, even, odd):
    return jnp.where(lax.axis_index(axis) % 2 == 0, even, odd)


def swap(values, axis, stride, mask):
    return lax.ppermute(values, axis, partners(axis, stride, mask))


def tree_sum(terms):
    while len(terms) > 1:
        terms = [terms[i] + terms[i + 1] for i in range(0, len(terms), 2)]
    return terms[0]


def first_sum_kernel(quarter, halo, keep_ref, got_ref, own_ref, ahead_ref, across_ref, behind_ref):
    rows = 4 * quarter + 3 * halo
    total = keep_ref[...] + got_ref[0:rows, :].astype(jnp.float32)
    spots = slot_rows(quarter, halo)
    own_ref[...] = total[:quarter]
    ahead_ref[...] = total[quarter : 2 * quarter + 3 * halo].astype(jnp.bfloat16)
    across_ref[...] = total[spots[2] : spots[2] + quarter].astype(jnp.bfloat16)
    behind_ref[...] = total[spots[3] : spots[3] + quarter].astype(jnp.bfloat16)


def second_sum_kernel(
    quarter,
    halo,
    own_ref,
    from_behind_ref,
    from_across_ref,
    from_ahead_ref,
    got_ref,
    halo_own_ref,
    mine_ref,
    along1_ref,
    along3_ref,
    middle_ref,
):
    f32, bf16 = jnp.float32, jnp.bfloat16
    index, odd_y = lax.axis_index("gx"), lax.axis_index("gy") & 1
    mine = (own_ref[...] + from_behind_ref[0:quarter, :].astype(f32)) + (
        from_across_ref[...].astype(f32) + from_ahead_ref[...].astype(f32)
    )
    mine = mine.astype(bf16)
    mine_ref[...] = mine
    far = from_behind_ref[quarter:, :].astype(f32)
    far = jnp.where((index == 0) | (index == 7), 0.0, far)
    strips = halo_own_ref[...].astype(f32) + got_ref[4 * quarter + 3 * halo :, :].astype(f32) + far
    low, high = strips[:halo].astype(bf16), strips[2 * halo :].astype(bf16)
    middle_ref[...] = strips[halo : 2 * halo]
    along3_ref[0:halo, :] = jnp.where(odd_y == 0, low, high)
    along3_ref[halo:, :] = mine
    along1_ref[0:halo, :] = jnp.where(odd_y == 0, high, low)
    along1_ref[halo:, :] = mine


def in_vmem(kernel, name, shapes, *operands):
    whole = pl.BlockSpec(memory_space=pltpu.VMEM)
    return pl.pallas_call(
        kernel,
        out_shape=tuple(pltpu.VMEM(shape, dtype) for shape, dtype in shapes),
        in_specs=[whole] * len(operands),
        out_specs=(whole,) * len(shapes),
        compiler_params=pltpu.CompilerParams(vmem_limit_bytes=8 * 1024 * 1024),
        name=name,
    )(*[pinned(operand) for operand in operands])


def sum_relayed(send, keep, halo_own, halo):
    f32, bf16 = jnp.float32, jnp.bfloat16
    width = send.shape[1]
    quarter = (send.shape[0] - 6 * halo) // 4
    index, row = lax.axis_index("gx"), lax.axis_index("gy")

    def turned(values, step):
        pairs = [(i, ((i >> 1) + step * (1 - 2 * (i & 1))) % 4 * 2 + (i & 1)) for i in range(8)]
        return lax.ppermute(values, "gx", pairs)

    got = swap(send, "gx", 1, 1)
    own, ahead, across, behind = in_vmem(
        functools.partial(first_sum_kernel, quarter, halo),
        "first_sum",
        (
            ((quarter, width), f32),
            ((quarter + 3 * halo, width), bf16),
            ((quarter, width), bf16),
            ((quarter, width), bf16),
        ),
        keep,
        got,
    )
    from_behind = turned(ahead, 1)
    from_ahead = turned(behind, 3)
    from_across = turned(across, 2)
    mine, to1, to3, middle = in_vmem(
        functools.partial(second_sum_kernel, quarter, halo),
        "second_sum",
        (
            ((quarter, width), bf16),
            ((quarter + halo, width), bf16),
            ((quarter + halo, width), bf16),
            ((halo, width), f32),
        ),
        own,
        from_behind,
        from_across,
        from_ahead,
        got,
        halo_own,
    )
    along3 = swap(to3, "gy", 1, 3)
    along2 = swap(mine, "gy", 1, 2)
    along1 = swap(to1, "gy", 1, 1)
    mine = tree_sum(
        [
            mine.astype(f32),
            along1[halo:].astype(f32),
            along2.astype(f32),
            along3[halo:].astype(f32),
        ]
    ).astype(bf16)
    last_far = jnp.where((row == 0) | (row == 3), bf16(0), along3[:halo])
    part3, part2, part1 = (swap(mine, "gx", 2, mask) for mask in (3, 2, 1))
    onward = ((index >> 1) & 1) == (index & 1)
    mine = jnp.concatenate(
        [mine, jnp.where(onward, part1, part3), part2, jnp.where(onward, part3, part1)]
    )
    return mine, swap(mine, "gx", 1, 1), middle, last_far, along1[:halo]


def sum_staged(send, keep, halo_own, halo):
    f32, bf16 = jnp.float32, jnp.bfloat16
    width = send.shape[1]
    quarter = (send.shape[0] - 6 * halo) // 4
    slots = slot_rows(quarter, halo)

    def joined_slots(values):
        return jnp.concatenate([values[spot : spot + quarter] for spot in slots])

    far = send[2 * quarter : 2 * quarter + 3 * halo]
    near = send[4 * quarter + 3 * halo :]
    back_far, back_near = pair_exchange(far, near, "gx")
    strips = halo_own.astype(f32) + back_far.astype(f32) + back_near.astype(f32)
    low, high = strips[:halo].astype(bf16), strips[2 * halo :].astype(bf16)
    last_far, last_near = pair_exchange(
        even_pick("gy", low, high), even_pick("gy", high, low), "gy"
    )
    index = lax.axis_index("gx")
    got = swap(joined_slots(send), "gx", 1, 1)
    total = (joined_slots(keep) + got.astype(f32)).astype(bf16)
    split = stages(lax.axis_size("gx"))[1:]
    for stride, factor in split:
        part = (index // stride) % factor
        height = total.shape[0] // factor
        mine = lax.dynamic_slice_in_dim(total, part * height, height, 0).astype(f32)
        for mask in range(factor - 1, 0, -1):
            piece = lax.dynamic_slice_in_dim(total, (part ^ mask) * height, height, 0)
            mine = mine + swap(piece, "gx", stride, mask).astype(f32)
        total = mine.astype(bf16)
    total = tree_sum(
        [total.astype(f32)]
        + [swap(total, "gy", 1, mask).astype(f32) for mask in range(1, lax.axis_size("gy"))]
    ).astype(bf16)
    for stride, factor in reversed(split):
        part = (index // stride) % factor
        height = total.shape[0]
        joined = jnp.zeros((factor * height, width), bf16)
        joined = lax.dynamic_update_slice_in_dim(joined, total, part * height, 0)
        for mask in range(factor - 1, 0, -1):
            piece = swap(total, "gx", stride, mask)
            joined = lax.dynamic_update_slice_in_dim(joined, piece, (part ^ mask) * height, 0)
        total = joined
    return total, swap(total, "gx", 1, 1), strips[halo : 2 * halo], last_far, last_near


def per_device(
    node_latents,
    edge_latents,
    node_cotangent,
    edge_cotangent,
    neighbours,
    edge_mask,
    send_table,
    counts,
    weights,
    vectors,
    weights_m,
    vectors_m,
    weights_v,
    vectors_v,
    weights_ema,
    vectors_ema,
):
    f32, bf16 = jnp.float32, jnp.bfloat16
    tok_rows, width = node_latents.shape
    halo = send_table.shape[1]
    boundary_pick = selector(send_table[0], tok_rows, bf16)
    boundary = jnp.dot(boundary_pick, node_latents, preferred_element_type=f32).astype(bf16)
    from_far, from_near = pair_exchange(boundary, boundary, "gx")
    ring = jnp.concatenate([from_far, from_near, boundary], axis=0)
    ring_far, ring_near = pair_exchange(ring, ring, "gy")
    unit = 16 * lax.axis_size("gx")
    grad_rows = -(-(weights.shape[0] * width + vectors.shape[0]) // unit) * unit
    relayed = lax.axis_size("gx") == 8 and lax.axis_size("gy") == 4
    edge_shape = (tok_rows * neighbours.shape[1] // CHUNK, CHUNK, width)
    plan = plan_call(
        halo, counts, neighbours, edge_mask, node_latents, vectors, node_cotangent, weights,
        edge_latents.reshape(edge_shape),
    )
    nodes_out, edges_out, edges_in_grad, node_part, halo_own, send, keep = layer_call(
        halo, relayed, grad_rows, ring, ring_far, ring_near, edge_cotangent.reshape(edge_shape),
        plan,
    )
    sums = sum_relayed if relayed else sum_staged
    mine, other, middle, last_far, last_near = sums(send, keep, halo_own, halo)
    boundary_grad = middle + last_far.astype(f32) + last_near.astype(f32)
    returned = lax.dot_general(
        boundary_pick.astype(f32),
        boundary_grad,
        (((0,), (0,)), ((), ())),
        precision=lax.Precision.HIGHEST,
        preferred_element_type=f32,
    )
    nodes_in_grad = (node_part + returned).astype(bf16)
    updated = update_call(
        relayed, mine, other, weights, vectors, weights_m, vectors_m, weights_v, vectors_v, weights_ema,
        vectors_ema,
    )
    return (
        nodes_out,
        edges_out.reshape(edge_latents.shape),
        nodes_in_grad,
        edges_in_grad.reshape(edge_latents.shape),
        updated[0].reshape(()),
    ) + tuple(updated[1:])


def solution(mesh):
    in_specs = (
        P(("gx", "gy"), None),
        P(("gx", "gy"), None, None),
        P(("gx", "gy"), None),
        P(("gx", "gy"), None, None),
        P(("gx", "gy"), None),
        P(("gx", "gy"), None),
        P(("gx", "gy"), None),
        P(("gx", "gy")),
        P(),
        P(),
        P(),
        P(),
        P(),
        P(),
        P(),
        P(),
    )
    out_specs = (
        P(("gx", "gy"), None),
        P(("gx", "gy"), None, None),
        P(("gx", "gy"), None),
        P(("gx", "gy"), None, None),
        P(),
        P(),
        P(),
        P(),
        P(),
        P(),
        P(),
        P(),
        P(),
        P(),
        P(),
    )
    return jax.shard_map(
        per_device, mesh=mesh, in_specs=in_specs, out_specs=out_specs, check_vma=False
    )
```

profile of v0, /device:TPU:0, one launch (start us, length us, event | category | flops | bytes accessed | tf_op | source)
XLA Modules:
  0.0 71.0 jit_solution(10025921203870239422)
XLA Ops:
  0.6 1.0 %convolution_convert_fusion = bf16[64,128]{1,0:T(8,128)(2,1)S(1)} fusion(bf16[256,128]{1,0:T(8,128)(2,1)} %latents_hbm.1, s32[64]{0:T(128)} %bitcast.13), kind=kOutput, calls=%fused_computation | convolution fusion | flops 4218880 | bytes 82176 | tf_op jit(solution)/shard_map/dot_general | solution.py:1070
  1.7 0.7 collective-permute-start
  2.4 4.4 %collective-permute-start.1 = (bf16[64,128]{1,0:T(8,128)(2,1)S(1)}, bf16[64,128]{1,0:T(8,128)(2,1)S(1)}, u32[]{:S(2)}, u32[]{:S(2)}) collective-permute-start(bf16[64,128]{1,0:T(8,128)(2,1)S(1)} %convolution_convert_fusion), channel_id=1, source_target_pairs={{0,4},{4,0},{8,12},{12,8},{16,20},{20,16},{24,28},{28,24},{1,5},{5... | collective-permute-start | bytes 49160 | tf_op jit(solution)/shard_map/ppermute | solution.py:866
  7.6 0.7 collective-permute-start.2
  8.2 4.5 %collective-permute-start.3 = (bf16[192,128]{1,0:T(8,128)(2,1)S(1)}, bf16[192,128]{1,0:T(8,128)(2,1)S(1)}, u32[]{:S(2)}, u32[]{:S(2)}) collective-permute-start(bf16[192,128]{1,0:T(8,128)(2,1)S(1)} %pad_maximum_fusion.1.ring_ref), channel_id=1, source_target_pairs={{0,1},{1,0},{2,3},{3,2},{4,5},{5,4},{6,7},{7,6},{8,9},{9,8},{10,11... | collective-permute-start | bytes 147464 | tf_op jit(solution)/shard_map/ppermute | solution.py:866
  12.7 2.6 %plan.1 = (bf16[256,128]{1,0:T(8,128)(2,1)S(1)}, f32[10,128]{1,0:T(8,128)S(1)}, bf16[256,128]{1,0:T(8,128)(2,1)S(1)}, bf16[1025,16,128]{2,1,0:T(8,128)(2,1)S(1)}...) custom-call(s32[1]{0:T(128)S(6)} %copy.35.count_ref, ...), custom_call_target="tpu_custom_call" | custom-call | flops 1000000000 | bytes 12000000 | tf_op jit(solution)/shard_map/plan/pallas_call | solution.py:648
  15.4 12.4 %edge_layer.1 = (bf16[256,128]{1,0:T(8,128)(2,1)}, bf16[1024,16,128]{2,1,0:T(8,128)(2,1)}, bf16[1024,16,128]{2,1,0:T(8,128)(2,1)}, f32[256,128]{1,0:T(8,128)S(1)...) custom-call(bf16[256,128]{1,0:T(8,128)(2,1)S(1)} %get-tuple-element., ...), custom_call_target="tpu_custom_call", output_to_operand_aliasing={{7}: (12, {}), {8}: (13, {})} | custom-call | tf_op jit(solution)/shard_map/edge_layer/pallas_call | solution.py:701
  27.8 1.5 %collective-permute-start.4 = (bf16[1024,128]{1,0:T(8,128)(2,1)S(1)}, bf16[1024,128]{1,0:T(8,128)(2,1)S(1)}, u32[]{:S(2)}, u32[]{:S(2)}) collective-permute-start(bf16[1024,128]{1,0:T(8,128)(2,1)S(1)} %get-tuple-element.67), channel_id=1, source_target_pairs={{0,4},{4,0},{8,12},{12,8},{16,20},{20,16},{24,28},{28,24},{1,5},{5... | collective-permute-start | bytes 786440 | tf_op jit(solution)/shard_map/ppermute | solution.py:878
  29.3 1.2 %collective-permute-done.4.got_ref = bf16[1024,128]{1,0:T(8,128)(2,1)S(1)} collective-permute-done((bf16[1024,128]{1,0:T(8,128)(2,1)S(1)}, bf16[1024,128]{1,0:T(8,128)(2,1)S(1)}, u32[]{:S(2)}, u32[]{:S(2)}) %collective-permute-start.4) | collective-permute-done | bytes 262176 | tf_op jit(solution)/shard_map/ppermute | solution.py:878
  30.5 3.8 %collective-permute-start.5 = (bf16[352,128]{1,0:T(8,128)(2,1)S(1)}, bf16[352,128]{1,0:T(8,128)(2,1)S(1)}, u32[]{:S(2)}, u32[]{:S(2)}) collective-permute-start(bf16[352,128]{1,0:T(8,128)(2,1)S(1)} %get-tuple-element.69), channel_id=1, source_target_pairs={{0,8},{4,28},{8,16},{12,4},{16,24},{20,12},{24,0},{28,20},{1,9},{5... | collective-permute-start | bytes 270344 | tf_op jit(solution)/shard_map/ppermute | solution.py:949
  34.4 7.4 %collective-permute-start.6 = (bf16[160,128]{1,0:T(8,128)(2,1)S(1)}, bf16[160,128]{1,0:T(8,128)(2,1)S(1)}, u32[]{:S(2)}, u32[]{:S(2)}) collective-permute-start(bf16[160,128]{1,0:T(8,128)(2,1)S(1)} %get-tuple-element.70), channel_id=1, source_target_pairs={{0,16},{4,20},{8,24},{12,28},{16,0},{20,4},{24,8},{28,12},{1,17},{... | collective-permute-start | bytes 122888 | tf_op jit(solution)/shard_map/ppermute | solution.py:949
  41.7 2.8 %collective-permute-done.6.from_across_ref = bf16[160,128]{1,0:T(8,128)(2,1)S(1)} collective-permute-done((bf16[160,128]{1,0:T(8,128)(2,1)S(1)}, bf16[160,128]{1,0:T(8,128)(2,1)S(1)}, u32[]{:S(2)}, u32[]{:S(2)}) %collective-permute-start.6) | collective-permute-done | bytes 40992 | tf_op jit(solution)/shard_map/ppermute | solution.py:949
  44.5 1.4 %collective-permute-done.7.from_ahead_ref = bf16[160,128]{1,0:T(8,128)(2,1)S(1)} collective-permute-done((bf16[160,128]{1,0:T(8,128)(2,1)S(1)}, bf16[160,128]{1,0:T(8,128)(2,1)S(1)}, u32[]{:S(2)}, u32[]{:S(2)}) %collective-permute-start.7) | collective-permute-done | bytes 40992 | tf_op jit(solution)/shard_map/ppermute | solution.py:949
  46.0 9.6 %collective-permute-start.8 = (bf16[224,128]{1,0:T(8,128)(2,1)S(1)}, bf16[224,128]{1,0:T(8,128)(2,1)S(1)}, u32[]{:S(2)}, u32[]{:S(2)}) collective-permute-start(bf16[224,128]{1,0:T(8,128)(2,1)S(1)} %get-tuple-element.74), channel_id=1, source_target_pairs={{0,3},{1,2},{2,1},{3,0},{4,7},{5,6},{6,5},{7,4},{8,11},{9,10},{10,... | collective-permute-start | bytes 172040 | tf_op jit(solution)/shard_map/ppermute | solution.py:878
  55.6 0.7 collective-permute-start.9
  56.3 4.9 %collective-permute-done.10 = bf16[160,128]{1,0:T(8,128)(2,1)S(1)} collective-permute-done((bf16[160,128]{1,0:T(8,128)(2,1)S(1)}, bf16[160,128]{1,0:T(8,128)(2,1)S(1)}, u32[]{:S(2)}, u32[]{:S(2)}) %collective-permute-start.10) | collective-permute-done | bytes 40992 | tf_op jit(solution)/shard_map/ppermute | solution.py:878
  61.2 1.0 %collective-permute-start.11 = (bf16[160,128]{1,0:T(8,128)(2,1)S(1)}, bf16[160,128]{1,0:T(8,128)(2,1)S(1)}, u32[]{:S(2)}, u32[]{:S(2)}) collective-permute-start(bf16[160,128]{1,0:T(8,128)(2,1)S(1)} %add_convert_fusion.1), channel_id=1, source_target_pairs={{0,8},{4,12},{8,0},{12,4},{16,24},{20,28},{24,16},{28,20},{1,9},{5... | collective-permute-start | bytes 122888 | tf_op jit(solution)/shard_map/ppermute | solution.py:878
  62.3 1.0 %collective-permute-start.12 = (bf16[160,128]{1,0:T(8,128)(2,1)S(1)}, bf16[160,128]{1,0:T(8,128)(2,1)S(1)}, u32[]{:S(2)}, u32[]{:S(2)}) collective-permute-start(bf16[160,128]{1,0:T(8,128)(2,1)S(1)} %add_convert_fusion.1), channel_id=1, source_target_pairs={{0,24},{4,28},{8,16},{12,20},{16,8},{20,12},{24,0},{28,4},{1,25},{... | collective-permute-start | bytes 122888 | tf_op jit(solution)/shard_map/ppermute | solution.py:878
  63.3 1.5 %collective-permute-start.13 = (bf16[160,128]{1,0:T(8,128)(2,1)S(1)}, bf16[160,128]{1,0:T(8,128)(2,1)S(1)}, u32[]{:S(2)}, u32[]{:S(2)}) collective-permute-start(bf16[160,128]{1,0:T(8,128)(2,1)S(1)} %add_convert_fusion.1), channel_id=1, source_target_pairs={{0,16},{4,20},{8,24},{12,28},{16,0},{20,4},{24,8},{28,12},{1,17},{... | collective-permute-start | bytes 122888 | tf_op jit(solution)/shard_map/ppermute | solution.py:878
  65.3 1.9 %collective-permute-done.12 = bf16[160,128]{1,0:T(8,128)(2,1)S(1)} collective-permute-done((bf16[160,128]{1,0:T(8,128)(2,1)S(1)}, bf16[160,128]{1,0:T(8,128)(2,1)S(1)}, u32[]{:S(2)}, u32[]{:S(2)}) %collective-permute-start.12) | collective-permute-done | bytes 40992 | tf_op jit(solution)/shard_map/ppermute | solution.py:878
  67.2 0.4 collective-permute-done.13
  67.7 0.7 add_convert_fusion
  68.3 0.7 %collective-permute-done.14.other_ref = bf16[640,128]{1,0:T(8,128)(2,1)S(1)} collective-permute-done((bf16[640,128]{1,0:T(8,128)(2,1)S(1)}, bf16[640,128]{1,0:T(8,128)(2,1)S(1)}, u32[]{:S(2)}, u32[]{:S(2)}) %collective-permute-start.14) | collective-permute-done | bytes 163872 | tf_op jit(solution)/shard_map/ppermute | solution.py:878
  69.1 1.8 %update.1 = (f32[1,1]{1,0:T(1,128)}, f32[9,128,128]{2,1,0:T(8,128)}, f32[10,128]{1,0:T(8,128)}, f32[9,128,128]{2,1,0:T(8,128)}, f32[10,128]{1,0:T(8,128)}, /*ind...) custom-call(bf16[640,128]{1,0:T(8,128)(2,1)S(1)} %pad_maximum_fusion, ...), custom_call_target="tpu_custom_call" | custom-call | tf_op jit(solution)/shard_map/update/pallas_call | solution.py:852
  (36 shorter events, 1.0 us)
Async XLA Ops:
  1.7 5.7 %collective-permute-start = (bf16[64,128]{1,0:T(8,128)(2,1)S(1)}, bf16[64,128]{1,0:T(8,128)(2,1)S(1)}, u32[]{:S(2)}, u32[]{:S(2)}) collective-permute-start(bf16[64,128]{1,0:T(8,128)(2,1)S(1)} %convolution_convert_fusion), channel_id=1, source_target_pairs={{4,8},{12,16},{20,24},{8,4},{16,12},{24,20},{5,9},{13,17},{21,25},... | collective-permute-start | bytes 49160 | tf_op jit(solution)/shard_map/ppermute | solution.py:866
  2.4 5.2 %collective-permute-start.1 = (bf16[64,128]{1,0:T(8,128)(2,1)S(1)}, bf16[64,128]{1,0:T(8,128)(2,1)S(1)}, u32[]{:S(2)}, u32[]{:S(2)}) collective-permute-start(bf16[64,128]{1,0:T(8,128)(2,1)S(1)} %convolution_convert_fusion), channel_id=1, source_target_pairs={{0,4},{4,0},{8,12},{12,8},{16,20},{20,16},{24,28},{28,24},{1,5},{5... | collective-permute-start | bytes 49160 | tf_op jit(solution)/shard_map/ppermute | solution.py:866
  7.6 7.7 %collective-permute-start.2 = (bf16[192,128]{1,0:T(8,128)(2,1)S(1)}, bf16[192,128]{1,0:T(8,128)(2,1)S(1)}, u32[]{:S(2)}, u32[]{:S(2)}) collective-permute-start(bf16[192,128]{1,0:T(8,128)(2,1)S(1)} %pad_maximum_fusion.1.ring_ref), channel_id=1, source_target_pairs={{1,2},{2,1},{5,6},{6,5},{9,10},{10,9},{13,14},{14,13},{17,18},{18,... | collective-permute-start | bytes 147464 | tf_op jit(solution)/shard_map/ppermute | solution.py:866
  8.2 7.1 %collective-permute-start.3 = (bf16[192,128]{1,0:T(8,128)(2,1)S(1)}, bf16[192,128]{1,0:T(8,128)(2,1)S(1)}, u32[]{:S(2)}, u32[]{:S(2)}) collective-permute-start(bf16[192,128]{1,0:T(8,128)(2,1)S(1)} %pad_maximum_fusion.1.ring_ref), channel_id=1, source_target_pairs={{0,1},{1,0},{2,3},{3,2},{4,5},{5,4},{6,7},{7,6},{8,9},{9,8},{10,11... | collective-permute-start | bytes 147464 | tf_op jit(solution)/shard_map/ppermute | solution.py:866
  15.3 49.4 %copy-start.8 = (s32[1,64]{1,0:T(1,128)S(1)}, s32[1,64]{1,0:T(1,128)}, u32[]{:S(2)}) copy-start(s32[1,64]{1,0:T(1,128)} %param.22) | copy-start | bytes 772
  15.3 53.7 %copy-start = (f32[9,128,128]{2,1,0:T(8,128)S(1)}, f32[9,128,128]{2,1,0:T(8,128)}, u32[]{:S(2)}) copy-start(f32[9,128,128]{2,1,0:T(8,128)} %weights_ref.1) | copy-start | bytes 1769476
  15.3 53.7 %copy-start.1 = (f32[9,128,128]{2,1,0:T(8,128)S(1)}, f32[9,128,128]{2,1,0:T(8,128)}, u32[]{:S(2)}) copy-start(f32[9,128,128]{2,1,0:T(8,128)} %weights_m_ref.1) | copy-start | bytes 1769476
  15.4 53.7 %copy-start.2 = (f32[9,128,128]{2,1,0:T(8,128)S(1)}, f32[9,128,128]{2,1,0:T(8,128)}, u32[]{:S(2)}) copy-start(f32[9,128,128]{2,1,0:T(8,128)} %weights_v_ref.1) | copy-start | bytes 1769476
  15.4 53.7 %copy-start.3 = (f32[9,128,128]{2,1,0:T(8,128)S(1)}, f32[9,128,128]{2,1,0:T(8,128)}, u32[]{:S(2)}) copy-start(f32[9,128,128]{2,1,0:T(8,128)} %weights_ema_ref.1) | copy-start | bytes 1769476
  15.4 53.7 %copy-start.4 = (f32[10,128]{1,0:T(8,128)S(1)}, f32[10,128]{1,0:T(8,128)}, u32[]{:S(2)}) copy-start(f32[10,128]{1,0:T(8,128)} %vectors_ref.1) | copy-start | bytes 15364
  15.4 53.7 %copy-start.5 = (f32[10,128]{1,0:T(8,128)S(1)}, f32[10,128]{1,0:T(8,128)}, u32[]{:S(2)}) copy-start(f32[10,128]{1,0:T(8,128)} %vectors_m_ref.1) | copy-start | bytes 15364
  15.4 53.7 %copy-start.6 = (f32[10,128]{1,0:T(8,128)S(1)}, f32[10,128]{1,0:T(8,128)}, u32[]{:S(2)}) copy-start(f32[10,128]{1,0:T(8,128)} %vectors_v_ref.1) | copy-start | bytes 15364
  15.4 53.7 %copy-start.7 = (f32[10,128]{1,0:T(8,128)S(1)}, f32[10,128]{1,0:T(8,128)}, u32[]{:S(2)}) copy-start(f32[10,128]{1,0:T(8,128)} %vectors_ema_ref.1) | copy-start | bytes 15364
  27.8 2.7 %collective-permute-start.4 = (bf16[1024,128]{1,0:T(8,128)(2,1)S(1)}, bf16[1024,128]{1,0:T(8,128)(2,1)S(1)}, u32[]{:S(2)}, u32[]{:S(2)}) collective-permute-start(bf16[1024,128]{1,0:T(8,128)(2,1)S(1)} %get-tuple-element.67), channel_id=1, source_target_pairs={{0,4},{4,0},{8,12},{12,8},{16,20},{20,16},{24,28},{28,24},{1,5},{5... | collective-permute-start | bytes 786440 | tf_op jit(solution)/shard_map/ppermute | solution.py:878
  30.5 15.4 %collective-permute-start.5 = (bf16[352,128]{1,0:T(8,128)(2,1)S(1)}, bf16[352,128]{1,0:T(8,128)(2,1)S(1)}, u32[]{:S(2)}, u32[]{:S(2)}) collective-permute-start(bf16[352,128]{1,0:T(8,128)(2,1)S(1)} %get-tuple-element.69), channel_id=1, source_target_pairs={{0,8},{4,28},{8,16},{12,4},{16,24},{20,12},{24,0},{28,20},{1,9},{5... | collective-permute-start | bytes 270344 | tf_op jit(solution)/shard_map/ppermute | solution.py:949
  34.4 10.2 %collective-permute-start.6 = (bf16[160,128]{1,0:T(8,128)(2,1)S(1)}, bf16[160,128]{1,0:T(8,128)(2,1)S(1)}, u32[]{:S(2)}, u32[]{:S(2)}) collective-permute-start(bf16[160,128]{1,0:T(8,128)(2,1)S(1)} %get-tuple-element.70), channel_id=1, source_target_pairs={{0,16},{4,20},{8,24},{12,28},{16,0},{20,4},{24,8},{28,12},{1,17},{... | collective-permute-start | bytes 122888 | tf_op jit(solution)/shard_map/ppermute | solution.py:949
  41.7 4.2 %collective-permute-start.7 = (bf16[160,128]{1,0:T(8,128)(2,1)S(1)}, bf16[160,128]{1,0:T(8,128)(2,1)S(1)}, u32[]{:S(2)}, u32[]{:S(2)}) collective-permute-start(bf16[160,128]{1,0:T(8,128)(2,1)S(1)} %get-tuple-element.71), channel_id=1, source_target_pairs={{0,24},{4,12},{8,0},{12,20},{16,8},{20,28},{24,16},{28,4},{1,25},{... | collective-permute-start | bytes 122888 | tf_op jit(solution)/shard_map/ppermute | solution.py:949
  46.0 15.2 %collective-permute-start.8 = (bf16[224,128]{1,0:T(8,128)(2,1)S(1)}, bf16[224,128]{1,0:T(8,128)(2,1)S(1)}, u32[]{:S(2)}, u32[]{:S(2)}) collective-permute-start(bf16[224,128]{1,0:T(8,128)(2,1)S(1)} %get-tuple-element.74), channel_id=1, source_target_pairs={{0,3},{1,2},{2,1},{3,0},{4,7},{5,6},{6,5},{7,4},{8,11},{9,10},{10,... | collective-permute-start | bytes 172040 | tf_op jit(solution)/shard_map/ppermute | solution.py:878
  55.6 5.6 %collective-permute-start.9 = (bf16[224,128]{1,0:T(8,128)(2,1)S(1)}, bf16[224,128]{1,0:T(8,128)(2,1)S(1)}, u32[]{:S(2)}, u32[]{:S(2)}) collective-permute-start(bf16[224,128]{1,0:T(8,128)(2,1)S(1)} %get-tuple-element.75), channel_id=1, source_target_pairs={{0,1},{1,0},{2,3},{3,2},{4,5},{5,4},{6,7},{7,6},{8,9},{9,8},{10,11... | collective-permute-start | bytes 172040 | tf_op jit(solution)/shard_map/ppermute | solution.py:878
  56.3 4.9 %collective-permute-start.10 = (bf16[160,128]{1,0:T(8,128)(2,1)S(1)}, bf16[160,128]{1,0:T(8,128)(2,1)S(1)}, u32[]{:S(2)}, u32[]{:S(2)}) collective-permute-start(bf16[160,128]{1,0:T(8,128)(2,1)S(1)} %get-tuple-element.77), channel_id=1, source_target_pairs={{0,2},{1,3},{2,0},{3,1},{4,6},{5,7},{6,4},{7,5},{8,10},{9,11},{10,... | collective-permute-start | bytes 122888 | tf_op jit(solution)/shard_map/ppermute | solution.py:878
  61.2 4.1 %collective-permute-start.11 = (bf16[160,128]{1,0:T(8,128)(2,1)S(1)}, bf16[160,128]{1,0:T(8,128)(2,1)S(1)}, u32[]{:S(2)}, u32[]{:S(2)}) collective-permute-start(bf16[160,128]{1,0:T(8,128)(2,1)S(1)} %add_convert_fusion.1), channel_id=1, source_target_pairs={{0,8},{4,12},{8,0},{12,4},{16,24},{20,28},{24,16},{28,20},{1,9},{5... | collective-permute-start | bytes 122888 | tf_op jit(solution)/shard_map/ppermute | solution.py:878
  62.3 4.9 %collective-permute-start.12 = (bf16[160,128]{1,0:T(8,128)(2,1)S(1)}, bf16[160,128]{1,0:T(8,128)(2,1)S(1)}, u32[]{:S(2)}, u32[]{:S(2)}) collective-permute-start(bf16[160,128]{1,0:T(8,128)(2,1)S(1)} %add_convert_fusion.1), channel_id=1, source_target_pairs={{0,24},{4,28},{8,16},{12,20},{16,8},{20,12},{24,0},{28,4},{1,25},{... | collective-permute-start | bytes 122888 | tf_op jit(solution)/shard_map/ppermute | solution.py:878
  63.3 4.3 %collective-permute-start.13 = (bf16[160,128]{1,0:T(8,128)(2,1)S(1)}, bf16[160,128]{1,0:T(8,128)(2,1)S(1)}, u32[]{:S(2)}, u32[]{:S(2)}) collective-permute-start(bf16[160,128]{1,0:T(8,128)(2,1)S(1)} %add_convert_fusion.1), channel_id=1, source_target_pairs={{0,16},{4,20},{8,24},{12,28},{16,0},{20,4},{24,8},{28,12},{1,17},{... | collective-permute-start | bytes 122888 | tf_op jit(solution)/shard_map/ppermute | solution.py:878
  67.6 1.5 %collective-permute-start.14 = (bf16[640,128]{1,0:T(8,128)(2,1)S(1)}, bf16[640,128]{1,0:T(8,128)(2,1)S(1)}, u32[]{:S(2)}, u32[]{:S(2)}) collective-permute-start(bf16[640,128]{1,0:T(8,128)(2,1)S(1)} %pad_maximum_fusion.mine_ref), channel_id=1, source_target_pairs={{0,4},{4,0},{8,12},{12,8},{16,20},{20,16},{24,28},{28,24},{1,5},{5... | collective-permute-start | bytes 491528 | tf_op jit(solution)/shard_map/ppermute | solution.py:878
where the time goes:
time: 69.9 us; the launch traced here: 71 us
  starting transfers between devices  36.8 us (53%)
  Pallas kernels  16.9 us (24%)
  waiting for transfers between devices  13.6 us (19%)
  between operations  1.52 us (2%)
  matrix products  1.41 us (2%)
  other arithmetic  0.71 us (1%)
    ppermute x8, starting transfers between devices, swap(): return lax.ppermute(values, axis, partners(axis, stride, mask))  15.4 us
    pallas_call x1, Pallas kernels, layer_call(): pl.pallas_call(functools.partial(layer_kernel, halo, relayed), out_shape=...  12.4 us
    ppermute x3, starting transfers between devices, turned(): return lax.ppermute(values, 'gx', pairs)  11.2 us
    ppermute x4, starting transfers between devices, pair_exchange(): return (lax.ppermute(to_far, axis, far), lax.ppermute(to_near, axis, near))  10.1 us
    ppermute x8, waiting for transfers between devices, swap(): return lax.ppermute(values, axis, partners(axis, stride, mask))  9.24 us
    ppermute x3, waiting for transfers between devices, turned(): return lax.ppermute(values, 'gx', pairs)  4.18 us
    pallas_call x1, Pallas kernels, plan_call(): pl.pallas_call(functools.partial(plan_kernel, halo), out_shape=(pltpu.VME...  2.59 us
    pallas_call x1, Pallas kernels, update_call(): pl.pallas_call(functools.partial(update_kernel, relayed), out_shape=tuple...  1.84 us
  transfers between devices with their start and end apart: 15, of which 9 were waited for; matrix products, arithmetic and copies ran while one was open for 1% of the time, Pallas kernels for 4%

commit v1 on v0

--- a/solution.py
+++ b/solution.py
@@ -300,6 +300,7 @@
     receiver_tile,
     chunk_sums,
     chunk_grads,
+    segment_acc,
     index_acc,
     mat_acc,
     vec_acc,
@@ -465,7 +466,21 @@
     for copy in stores:
         copy.start()
 
-    aggregate = halves(dot(segment_ref[...], split_pair(chunk_sums[0:chunks, :]))).astype(bf16)
+    def segment_sum(part):
+        half, most = chunks // 2, 3 * chunks // 4
+        segment_acc[...] = part(0, half)
+        for low, high in ((half, most), (most, chunks)):
+
+            @pl.when(listed[3, 0] > low)
+            def _():
+                segment_acc[...] += part(low, high)
+
+        return halves(segment_acc[...])
+
+    def forward_part(low, high):
+        return dot(segment_ref[:, low:high], split_pair(chunk_sums[low:high, :]))
+
+    aggregate = segment_sum(forward_part).astype(bf16)
     half1 = 0.5 * (dot(latents, low_ref[5]) + dot(aggregate, low_ref[6]) + vector(5))
     act1, slope1 = silu_of_half(half1)
     act1 = act1.astype(bf16)
@@ -565,12 +580,22 @@
     def last_tile(p):
         return (listed[4, (p + 1) * (piece // per) - 1] + (GROUP - 1)) >> 5
 
+    def has_live(p):
+        before = listed[4, jnp.maximum(p * (piece // per) - 1, 0)]
+        return jnp.where(p == 0, 0, before) < listed[3, 0]
+
+    @pl.loop(0, PIECES)
+    def _(p):
+        @pl.when(jnp.logical_not(has_live(p)))
+        def _():
+            send_piece(p)
+
     def backward_piece(p, t):
         upto = last_tile(p) + 1
         stop = jnp.minimum(upto, tiles)
         lax.fori_loop(t, stop, backward, 0)
 
-        @pl.when(upto <= tiles)
+        @pl.when((upto <= tiles) & has_live(p))
         def _():
             send_piece(p)
 
@@ -581,15 +606,17 @@
 
     @pl.loop(0, PIECES)
     def _(p):
-        @pl.when(last_tile(p) + 1 > tiles)
+        @pl.when((last_tile(p) + 1 > tiles) & has_live(p))
         def _():
             send_piece(p)
 
-    stacked = split_pair(
-        jnp.concatenate([chunk_grads[g] for g in range(chunks // LANES)], axis=1), axis=0
-    )
-    receiver_grad = halves(dot_nt(segment_ref[...], stacked)).astype(bf16)
-    grads[tail : tail + 1, :] = halves(dot_nt(jnp.ones((8, chunks), bf16), stacked))[0:1, :]
+    def backward_part(low, high):
+        groups = [chunk_grads[g] for g in range(low // LANES, high // LANES)]
+        return dot_nt(segment_ref[:, low:high], split_pair(jnp.concatenate(groups, axis=1), axis=0))
+
+    receiver_grad = segment_sum(backward_part)
+    grads[tail : tail + 1, :] = column_total(receiver_grad)
+    receiver_grad = receiver_grad.astype(bf16)
     for row in range(1, 5):
         values = column_total(vec_acc[8 * row : 8 * row + 8, :])
         grads[tail + row : tail + row + 1, :] = values * root if row == 3 else values
@@ -730,6 +757,7 @@
             pltpu.VMEM((GROUP, width), f32),
             pltpu.VMEM((chunks + GROUP, width), f32),
             pltpu.VMEM((chunks // LANES + 1, width, LANES), f32),
+            pltpu.VMEM((particles, 2 * width), f32),
             pltpu.VMEM((width, rows + width), f32),
             pltpu.VMEM((2, width, width), f32),
             pltpu.VMEM((40, width), f32),

time: 69.9 us -> 71 us (1.016)
  Pallas kernels: 16.9 us -> 19 us
    pallas_call x1, Pallas kernels: 12.4 us -> 14.5 us  [layer_call(): pl.pallas_call(functools.partial(layer_kernel, halo, relayed), out_shape=...]
    ppermute x3, starting transfers between devices: 11.2 us -> 9.72 us  [turned(): return lax.ppermute(values, 'gx', pairs)]
    ppermute x8, starting transfers between devices: 15.4 us -> 16.7 us  [swap(): return lax.ppermute(values, axis, partners(axis, stride, mask))]
where the time goes in v1:
time: 71 us; the launch traced here: 72.2 us
  starting transfers between devices  36.5 us (51%)
  Pallas kernels  19 us (27%)
  waiting for transfers between devices  13 us (18%)
  between operations  1.54 us (2%)
  matrix products  1.41 us (2%)
  other arithmetic  0.71 us (1%)
    ppermute x8, starting transfers between devices, swap(): return lax.ppermute(values, axis, partners(axis, stride, mask))  16.7 us
    pallas_call x1, Pallas kernels, layer_call(): pl.pallas_call(functools.partial(layer_kernel, halo, relayed), out_shape=...  14.5 us
    ppermute x4, starting transfers between devices, pair_exchange(): return (lax.ppermute(to_far, axis, far), lax.ppermute(to_near, axis, near))  10.1 us
    ppermute x3, starting transfers between devices, turned(): return lax.ppermute(values, 'gx', pairs)  9.72 us
    ppermute x8, waiting for transfers between devices, swap(): return lax.ppermute(values, axis, partners(axis, stride, mask))  8.79 us
    ppermute x3, waiting for transfers between devices, turned(): return lax.ppermute(values, 'gx', pairs)  4 us
    pallas_call x1, Pallas kernels, plan_call(): pl.pallas_call(functools.partial(plan_kernel, halo), out_shape=(pltpu.VME...  2.59 us
    pallas_call x1, Pallas kernels, update_call(): pl.pallas_call(functools.partial(update_kernel, relayed), out_shape=tuple...  1.84 us
  transfers between devices with their start and end apart: 15, of which 9 were waited for; matrix products, arithmetic and copies ran while one was open for 1% of the time, Pallas kernels for 4%

profile of v1, /device:TPU:0, one launch (start us, length us, event | category | flops | bytes accessed | tf_op | source)
XLA Modules:
  0.0 72.2 jit_solution(999103450431705888)
XLA Ops:
  0.6 1.0 %convolution_convert_fusion = bf16[64,128]{1,0:T(8,128)(2,1)S(1)} fusion(bf16[256,128]{1,0:T(8,128)(2,1)} %latents_hbm.1, s32[64]{0:T(128)} %bitcast.13), kind=kOutput, calls=%fused_computation | convolution fusion | flops 4218880 | bytes 82176 | tf_op jit(solution)/shard_map/dot_general | solution.py:1098
  1.7 0.7 collective-permute-start
  2.4 4.4 %collective-permute-start.1 = (bf16[64,128]{1,0:T(8,128)(2,1)S(1)}, bf16[64,128]{1,0:T(8,128)(2,1)S(1)}, u32[]{:S(2)}, u32[]{:S(2)}) collective-permute-start(bf16[64,128]{1,0:T(8,128)(2,1)S(1)} %convolution_convert_fusion), channel_id=1, source_target_pairs={{0,4},{4,0},{8,12},{12,8},{16,20},{20,16},{24,28},{28,24},{1,5},{5... | collective-permute-start | bytes 49160 | tf_op jit(solution)/shard_map/ppermute | solution.py:894
  7.4 0.2 collective-permute-done.1
  7.6 0.7 collective-permute-start.2
  8.2 4.5 %collective-permute-start.3 = (bf16[192,128]{1,0:T(8,128)(2,1)S(1)}, bf16[192,128]{1,0:T(8,128)(2,1)S(1)}, u32[]{:S(2)}, u32[]{:S(2)}) collective-permute-start(bf16[192,128]{1,0:T(8,128)(2,1)S(1)} %pad_maximum_fusion.1.ring_ref), channel_id=1, source_target_pairs={{0,1},{1,0},{2,3},{3,2},{4,5},{5,4},{6,7},{7,6},{8,9},{9,8},{10,11... | collective-permute-start | bytes 147464 | tf_op jit(solution)/shard_map/ppermute | solution.py:894
  12.7 2.6 %plan.1 = (bf16[256,128]{1,0:T(8,128)(2,1)S(1)}, f32[10,128]{1,0:T(8,128)S(1)}, bf16[256,128]{1,0:T(8,128)(2,1)S(1)}, bf16[1025,16,128]{2,1,0:T(8,128)(2,1)S(1)}...) custom-call(s32[1]{0:T(128)S(6)} %copy.35.count_ref, ...), custom_call_target="tpu_custom_call" | custom-call | flops 1000000000 | bytes 12000000 | tf_op jit(solution)/shard_map/plan/pallas_call | solution.py:675
  15.4 14.5 %edge_layer.1 = (bf16[256,128]{1,0:T(8,128)(2,1)}, bf16[1024,16,128]{2,1,0:T(8,128)(2,1)}, bf16[1024,16,128]{2,1,0:T(8,128)(2,1)}, f32[256,128]{1,0:T(8,128)S(1)...) custom-call(bf16[256,128]{1,0:T(8,128)(2,1)S(1)} %get-tuple-element., ...), custom_call_target="tpu_custom_call", output_to_operand_aliasing={{7}: (12, {}), {8}: (13, {})} | custom-call | tf_op jit(solution)/shard_map/edge_layer/pallas_call | solution.py:728
  30.0 1.5 %collective-permute-done.4.got_ref = bf16[1024,128]{1,0:T(8,128)(2,1)S(1)} collective-permute-done((bf16[1024,128]{1,0:T(8,128)(2,1)S(1)}, bf16[1024,128]{1,0:T(8,128)(2,1)S(1)}, u32[]{:S(2)}, u32[]{:S(2)}) %collective-permute-start.4) | collective-permute-done | bytes 262176 | tf_op jit(solution)/shard_map/ppermute | solution.py:906
  31.6 9.7 %collective-permute-start.6 = (bf16[160,128]{1,0:T(8,128)(2,1)S(1)}, bf16[160,128]{1,0:T(8,128)(2,1)S(1)}, u32[]{:S(2)}, u32[]{:S(2)}) collective-permute-start(bf16[160,128]{1,0:T(8,128)(2,1)S(1)} %get-tuple-element.70), channel_id=1, source_target_pairs={{0,16},{4,20},{8,24},{12,28},{16,0},{20,4},{24,8},{28,12},{1,17},{... | collective-permute-start | bytes 122888 | tf_op jit(solution)/shard_map/ppermute | solution.py:977
  41.3 3.2 %collective-permute-done.6.from_across_ref = bf16[160,128]{1,0:T(8,128)(2,1)S(1)} collective-permute-done((bf16[160,128]{1,0:T(8,128)(2,1)S(1)}, bf16[160,128]{1,0:T(8,128)(2,1)S(1)}, u32[]{:S(2)}, u32[]{:S(2)}) %collective-permute-start.6) | collective-permute-done | bytes 40992 | tf_op jit(solution)/shard_map/ppermute | solution.py:977
  44.5 0.8 %collective-permute-done.7.from_ahead_ref = bf16[160,128]{1,0:T(8,128)(2,1)S(1)} collective-permute-done((bf16[160,128]{1,0:T(8,128)(2,1)S(1)}, bf16[160,128]{1,0:T(8,128)(2,1)S(1)}, u32[]{:S(2)}, u32[]{:S(2)}) %collective-permute-start.7) | collective-permute-done | bytes 40992 | tf_op jit(solution)/shard_map/ppermute | solution.py:977
  45.4 12.3 %collective-permute-start.8 = (bf16[224,128]{1,0:T(8,128)(2,1)S(1)}, bf16[224,128]{1,0:T(8,128)(2,1)S(1)}, u32[]{:S(2)}, u32[]{:S(2)}) collective-permute-start(bf16[224,128]{1,0:T(8,128)(2,1)S(1)} %get-tuple-element.74), channel_id=1, source_target_pairs={{0,3},{1,2},{2,1},{3,0},{4,7},{5,6},{6,5},{7,4},{8,11},{9,10},{10,... | collective-permute-start | bytes 172040 | tf_op jit(solution)/shard_map/ppermute | solution.py:906
  57.7 0.6 collective-permute-start.10
  58.3 4.3 %collective-permute-done.10 = bf16[160,128]{1,0:T(8,128)(2,1)S(1)} collective-permute-done((bf16[160,128]{1,0:T(8,128)(2,1)S(1)}, bf16[160,128]{1,0:T(8,128)(2,1)S(1)}, u32[]{:S(2)}, u32[]{:S(2)}) %collective-permute-start.10) | collective-permute-done | bytes 40992 | tf_op jit(solution)/shard_map/ppermute | solution.py:906
  62.6 0.9 %collective-permute-start.11 = (bf16[160,128]{1,0:T(8,128)(2,1)S(1)}, bf16[160,128]{1,0:T(8,128)(2,1)S(1)}, u32[]{:S(2)}, u32[]{:S(2)}) collective-permute-start(bf16[160,128]{1,0:T(8,128)(2,1)S(1)} %add_convert_fusion.1), channel_id=1, source_target_pairs={{0,8},{4,12},{8,0},{12,4},{16,24},{20,28},{24,16},{28,20},{1,9},{5... | collective-permute-start | bytes 122888 | tf_op jit(solution)/shard_map/ppermute | solution.py:906
  63.5 1.2 %collective-permute-start.12 = (bf16[160,128]{1,0:T(8,128)(2,1)S(1)}, bf16[160,128]{1,0:T(8,128)(2,1)S(1)}, u32[]{:S(2)}, u32[]{:S(2)}) collective-permute-start(bf16[160,128]{1,0:T(8,128)(2,1)S(1)} %add_convert_fusion.1), channel_id=1, source_target_pairs={{0,24},{4,28},{8,16},{12,20},{16,8},{20,12},{24,0},{28,4},{1,25},{... | collective-permute-start | bytes 122888 | tf_op jit(solution)/shard_map/ppermute | solution.py:906
  64.7 1.5 %collective-permute-start.13 = (bf16[160,128]{1,0:T(8,128)(2,1)S(1)}, bf16[160,128]{1,0:T(8,128)(2,1)S(1)}, u32[]{:S(2)}, u32[]{:S(2)}) collective-permute-start(bf16[160,128]{1,0:T(8,128)(2,1)S(1)} %add_convert_fusion.1), channel_id=1, source_target_pairs={{0,16},{4,20},{8,24},{12,28},{16,0},{20,4},{24,8},{28,12},{1,17},{... | collective-permute-start | bytes 122888 | tf_op jit(solution)/shard_map/ppermute | solution.py:906
  66.2 0.4 fusion
  66.7 1.7 %collective-permute-done.12 = bf16[160,128]{1,0:T(8,128)(2,1)S(1)} collective-permute-done((bf16[160,128]{1,0:T(8,128)(2,1)S(1)}, bf16[160,128]{1,0:T(8,128)(2,1)S(1)}, u32[]{:S(2)}, u32[]{:S(2)}) %collective-permute-start.12) | collective-permute-done | bytes 40992 | tf_op jit(solution)/shard_map/ppermute | solution.py:906
  68.4 0.4 collective-permute-done.13
  68.9 0.7 add_convert_fusion
  69.6 0.7 %collective-permute-done.14.other_ref = bf16[640,128]{1,0:T(8,128)(2,1)S(1)} collective-permute-done((bf16[640,128]{1,0:T(8,128)(2,1)S(1)}, bf16[640,128]{1,0:T(8,128)(2,1)S(1)}, u32[]{:S(2)}, u32[]{:S(2)}) %collective-permute-start.14) | collective-permute-done | bytes 163872 | tf_op jit(solution)/shard_map/ppermute | solution.py:906
  70.4 1.8 %update.1 = (f32[1,1]{1,0:T(1,128)}, f32[9,128,128]{2,1,0:T(8,128)}, f32[10,128]{1,0:T(8,128)}, f32[9,128,128]{2,1,0:T(8,128)}, f32[10,128]{1,0:T(8,128)}, /*ind...) custom-call(bf16[640,128]{1,0:T(8,128)(2,1)S(1)} %pad_maximum_fusion, ...), custom_call_target="tpu_custom_call" | custom-call | tf_op jit(solution)/shard_map/update/pallas_call | solution.py:880
  (36 shorter events, 0.6 us)
Async XLA Ops:
  1.7 5.7 %collective-permute-start = (bf16[64,128]{1,0:T(8,128)(2,1)S(1)}, bf16[64,128]{1,0:T(8,128)(2,1)S(1)}, u32[]{:S(2)}, u32[]{:S(2)}) collective-permute-start(bf16[64,128]{1,0:T(8,128)(2,1)S(1)} %convolution_convert_fusion), channel_id=1, source_target_pairs={{4,8},{12,16},{20,24},{8,4},{16,12},{24,20},{5,9},{13,17},{21,25},... | collective-permute-start | bytes 49160 | tf_op jit(solution)/shard_map/ppermute | solution.py:894
  2.4 5.2 %collective-permute-start.1 = (bf16[64,128]{1,0:T(8,128)(2,1)S(1)}, bf16[64,128]{1,0:T(8,128)(2,1)S(1)}, u32[]{:S(2)}, u32[]{:S(2)}) collective-permute-start(bf16[64,128]{1,0:T(8,128)(2,1)S(1)} %convolution_convert_fusion), channel_id=1, source_target_pairs={{0,4},{4,0},{8,12},{12,8},{16,20},{20,16},{24,28},{28,24},{1,5},{5... | collective-permute-start | bytes 49160 | tf_op jit(solution)/shard_map/ppermute | solution.py:894
  7.6 7.7 %collective-permute-start.2 = (bf16[192,128]{1,0:T(8,128)(2,1)S(1)}, bf16[192,128]{1,0:T(8,128)(2,1)S(1)}, u32[]{:S(2)}, u32[]{:S(2)}) collective-permute-start(bf16[192,128]{1,0:T(8,128)(2,1)S(1)} %pad_maximum_fusion.1.ring_ref), channel_id=1, source_target_pairs={{1,2},{2,1},{5,6},{6,5},{9,10},{10,9},{13,14},{14,13},{17,18},{18,... | collective-permute-start | bytes 147464 | tf_op jit(solution)/shard_map/ppermute | solution.py:894
  8.2 7.1 %collective-permute-start.3 = (bf16[192,128]{1,0:T(8,128)(2,1)S(1)}, bf16[192,128]{1,0:T(8,128)(2,1)S(1)}, u32[]{:S(2)}, u32[]{:S(2)}) collective-permute-start(bf16[192,128]{1,0:T(8,128)(2,1)S(1)} %pad_maximum_fusion.1.ring_ref), channel_id=1, source_target_pairs={{0,1},{1,0},{2,3},{3,2},{4,5},{5,4},{6,7},{7,6},{8,9},{9,8},{10,11... | collective-permute-start | bytes 147464 | tf_op jit(solution)/shard_map/ppermute | solution.py:894
  15.3 50.9 %copy-start.8 = (s32[1,64]{1,0:T(1,128)S(1)}, s32[1,64]{1,0:T(1,128)}, u32[]{:S(2)}) copy-start(s32[1,64]{1,0:T(1,128)} %param.22) | copy-start | bytes 772
  15.3 55.0 %copy-start = (f32[9,128,128]{2,1,0:T(8,128)S(1)}, f32[9,128,128]{2,1,0:T(8,128)}, u32[]{:S(2)}) copy-start(f32[9,128,128]{2,1,0:T(8,128)} %weights_ref.1) | copy-start | bytes 1769476
  15.3 55.0 %copy-start.1 = (f32[9,128,128]{2,1,0:T(8,128)S(1)}, f32[9,128,128]{2,1,0:T(8,128)}, u32[]{:S(2)}) copy-start(f32[9,128,128]{2,1,0:T(8,128)} %weights_m_ref.1) | copy-start | bytes 1769476
  15.4 55.0 %copy-start.2 = (f32[9,128,128]{2,1,0:T(8,128)S(1)}, f32[9,128,128]{2,1,0:T(8,128)}, u32[]{:S(2)}) copy-start(f32[9,128,128]{2,1,0:T(8,128)} %weights_v_ref.1) | copy-start | bytes 1769476
  15.4 55.0 %copy-start.3 = (f32[9,128,128]{2,1,0:T(8,128)S(1)}, f32[9,128,128]{2,1,0:T(8,128)}, u32[]{:S(2)}) copy-start(f32[9,128,128]{2,1,0:T(8,128)} %weights_ema_ref.1) | copy-start | bytes 1769476
  15.4 55.0 %copy-start.4 = (f32[10,128]{1,0:T(8,128)S(1)}, f32[10,128]{1,0:T(8,128)}, u32[]{:S(2)}) copy-start(f32[10,128]{1,0:T(8,128)} %vectors_ref.1) | copy-start | bytes 15364
  15.4 55.0 %copy-start.5 = (f32[10,128]{1,0:T(8,128)S(1)}, f32[10,128]{1,0:T(8,128)}, u32[]{:S(2)}) copy-start(f32[10,128]{1,0:T(8,128)} %vectors_m_ref.1) | copy-start | bytes 15364
  15.4 55.0 %copy-start.6 = (f32[10,128]{1,0:T(8,128)S(1)}, f32[10,128]{1,0:T(8,128)}, u32[]{:S(2)}) copy-start(f32[10,128]{1,0:T(8,128)} %vectors_v_ref.1) | copy-start | bytes 15364
  15.4 55.0 %copy-start.7 = (f32[10,128]{1,0:T(8,128)S(1)}, f32[10,128]{1,0:T(8,128)}, u32[]{:S(2)}) copy-start(f32[10,128]{1,0:T(8,128)} %vectors_ema_ref.1) | copy-start | bytes 15364
  29.9 1.6 %collective-permute-start.4 = (bf16[1024,128]{1,0:T(8,128)(2,1)S(1)}, bf16[1024,128]{1,0:T(8,128)(2,1)S(1)}, u32[]{:S(2)}, u32[]{:S(2)}) collective-permute-start(bf16[1024,128]{1,0:T(8,128)(2,1)S(1)} %get-tuple-element.67), channel_id=1, source_target_pairs={{0,4},{4,0},{8,12},{12,8},{16,20},{20,16},{24,28},{28,24},{1,5},{5... | collective-permute-start | bytes 786440 | tf_op jit(solution)/shard_map/ppermute | solution.py:906
  31.6 13.7 %collective-permute-start.5 = (bf16[352,128]{1,0:T(8,128)(2,1)S(1)}, bf16[352,128]{1,0:T(8,128)(2,1)S(1)}, u32[]{:S(2)}, u32[]{:S(2)}) collective-permute-start(bf16[352,128]{1,0:T(8,128)(2,1)S(1)} %get-tuple-element.69), channel_id=1, source_target_pairs={{0,8},{4,28},{8,16},{12,4},{16,24},{20,12},{24,0},{28,20},{1,9},{5... | collective-permute-start | bytes 270344 | tf_op jit(solution)/shard_map/ppermute | solution.py:977
  31.6 12.9 %collective-permute-start.6 = (bf16[160,128]{1,0:T(8,128)(2,1)S(1)}, bf16[160,128]{1,0:T(8,128)(2,1)S(1)}, u32[]{:S(2)}, u32[]{:S(2)}) collective-permute-start(bf16[160,128]{1,0:T(8,128)(2,1)S(1)} %get-tuple-element.70), channel_id=1, source_target_pairs={{0,16},{4,20},{8,24},{12,28},{16,0},{20,4},{24,8},{28,12},{1,17},{... | collective-permute-start | bytes 122888 | tf_op jit(solution)/shard_map/ppermute | solution.py:977
  41.3 4.0 %collective-permute-start.7 = (bf16[160,128]{1,0:T(8,128)(2,1)S(1)}, bf16[160,128]{1,0:T(8,128)(2,1)S(1)}, u32[]{:S(2)}, u32[]{:S(2)}) collective-permute-start(bf16[160,128]{1,0:T(8,128)(2,1)S(1)} %get-tuple-element.71), channel_id=1, source_target_pairs={{0,24},{4,12},{8,0},{12,20},{16,8},{20,28},{24,16},{28,4},{1,25},{... | collective-permute-start | bytes 122888 | tf_op jit(solution)/shard_map/ppermute | solution.py:977
  45.4 17.2 %collective-permute-start.8 = (bf16[224,128]{1,0:T(8,128)(2,1)S(1)}, bf16[224,128]{1,0:T(8,128)(2,1)S(1)}, u32[]{:S(2)}, u32[]{:S(2)}) collective-permute-start(bf16[224,128]{1,0:T(8,128)(2,1)S(1)} %get-tuple-element.74), channel_id=1, source_target_pairs={{0,3},{1,2},{2,1},{3,0},{4,7},{5,6},{6,5},{7,4},{8,11},{9,10},{10,... | collective-permute-start | bytes 172040 | tf_op jit(solution)/shard_map/ppermute | solution.py:906
  57.7 4.9 %collective-permute-start.9 = (bf16[224,128]{1,0:T(8,128)(2,1)S(1)}, bf16[224,128]{1,0:T(8,128)(2,1)S(1)}, u32[]{:S(2)}, u32[]{:S(2)}) collective-permute-start(bf16[224,128]{1,0:T(8,128)(2,1)S(1)} %get-tuple-element.75), channel_id=1, source_target_pairs={{0,1},{1,0},{2,3},{3,2},{4,5},{5,4},{6,7},{7,6},{8,9},{9,8},{10,11... | collective-permute-start | bytes 172040 | tf_op jit(solution)/shard_map/ppermute | solution.py:906
  57.7 4.9 %collective-permute-start.10 = (bf16[160,128]{1,0:T(8,128)(2,1)S(1)}, bf16[160,128]{1,0:T(8,128)(2,1)S(1)}, u32[]{:S(2)}, u32[]{:S(2)}) collective-permute-start(bf16[160,128]{1,0:T(8,128)(2,1)S(1)} %get-tuple-element.77), channel_id=1, source_target_pairs={{0,2},{1,3},{2,0},{3,1},{4,6},{5,7},{6,4},{7,5},{8,10},{9,11},{10,... | collective-permute-start | bytes 122888 | tf_op jit(solution)/shard_map/ppermute | solution.py:906
  62.6 4.1 %collective-permute-start.11 = (bf16[160,128]{1,0:T(8,128)(2,1)S(1)}, bf16[160,128]{1,0:T(8,128)(2,1)S(1)}, u32[]{:S(2)}, u32[]{:S(2)}) collective-permute-start(bf16[160,128]{1,0:T(8,128)(2,1)S(1)} %add_convert_fusion.1), channel_id=1, source_target_pairs={{0,8},{4,12},{8,0},{12,4},{16,24},{20,28},{24,16},{28,20},{1,9},{5... | collective-permute-start | bytes 122888 | tf_op jit(solution)/shard_map/ppermute | solution.py:906
  63.5 4.9 %collective-permute-start.12 = (bf16[160,128]{1,0:T(8,128)(2,1)S(1)}, bf16[160,128]{1,0:T(8,128)(2,1)S(1)}, u32[]{:S(2)}, u32[]{:S(2)}) collective-permute-start(bf16[160,128]{1,0:T(8,128)(2,1)S(1)} %add_convert_fusion.1), channel_id=1, source_target_pairs={{0,24},{4,28},{8,16},{12,20},{16,8},{20,12},{24,0},{28,4},{1,25},{... | collective-permute-start | bytes 122888 | tf_op jit(solution)/shard_map/ppermute | solution.py:906
  64.7 4.2 %collective-permute-start.13 = (bf16[160,128]{1,0:T(8,128)(2,1)S(1)}, bf16[160,128]{1,0:T(8,128)(2,1)S(1)}, u32[]{:S(2)}, u32[]{:S(2)}) collective-permute-start(bf16[160,128]{1,0:T(8,128)(2,1)S(1)} %add_convert_fusion.1), channel_id=1, source_target_pairs={{0,16},{4,20},{8,24},{12,28},{16,0},{20,4},{24,8},{28,12},{1,17},{... | collective-permute-start | bytes 122888 | tf_op jit(solution)/shard_map/ppermute | solution.py:906
  68.9 1.5 %collective-permute-start.14 = (bf16[640,128]{1,0:T(8,128)(2,1)S(1)}, bf16[640,128]{1,0:T(8,128)(2,1)S(1)}, u32[]{:S(2)}, u32[]{:S(2)}) collective-permute-start(bf16[640,128]{1,0:T(8,128)(2,1)S(1)} %pad_maximum_fusion.mine_ref), channel_id=1, source_target_pairs={{0,4},{4,0},{8,12},{12,8},{16,20},{20,16},{24,28},{28,24},{1,5},{5... | collective-permute-start | bytes 491528 | tf_op jit(solution)/shard_map/ppermute | solution.py:906
